TPU v7x, 256 devices: a whole 4x4x8 slice. The times are simulated.
256 devices in a mesh: dp: 64 (over x_lo, y, z), group: 4 (over x_hi, core).
Axes of the slice: x: 4 (x_hi: 2, x_lo: 2; x = x_hi * 2 + x_lo), y: 4, z: 8, core: 2. Of those that a mesh axis runs over, the one named last changes fastest.
Arguments:
- event: bfloat16 [12288, 1024], P('dp'), may hold values from -0.1875 to 0.1875
- lidar: bfloat16 [12288, 1024], P('dp'), may hold values from -0.1875 to 0.1875
- frame: bfloat16 [12288, 1024], P('dp'), may hold values from -0.1875 to 0.1875
- sample_ids: int32 [3, 12288], replicated, may hold values from 0 to 12287, each once within a row
- logit_scale: float32 [3], replicated, may hold values from 10 to 40
- logit_bias: float32 [3], replicated, may hold values from -4 to -1
Outputs:
- grad_event: float32 [12288, 1024], P('dp')
- grad_lidar: float32 [12288, 1024], P('dp')
- grad_frame: float32 [12288, 1024], P('dp')
Inputs may be any that keep to these rules, and one draw needn't show every extreme that they name: Each row of sample_ids is a permutation of 0 to 12287, so every row has exactly one partner of its sample in each other modality.
All inputs are finite; a program needn't handle non-finite values.
Results may differ from a plain program's by a relative error of at most 0.0015.
Values may be sent and summed in bfloat16 or wider, within the bound.
A program may use at most 128 MiB of HBM per device.

v0:
```python
import jax
import jax.numpy as jnp
from jax import lax
from jax.sharding import PartitionSpec as P


def coefs(left, right, left_ids, right_ids, scale, bias):
    logits = jnp.einsum("id,jd->ij", left, right, preferred_element_type=jnp.float32)
    labels = (left_ids[:, None] == right_ids[None, :]).astype(jnp.float32)
    return (jax.nn.sigmoid(scale * logits + bias) - labels).astype(jnp.bfloat16)


def body(event, lidar, frame, sample_ids, logit_scale, logit_bias):
    rows = event.shape[0]
    width = event.shape[1]
    ranks = lax.axis_size("dp")
    members = lax.axis_size("group")
    quarter = rows // members
    here = lax.axis_index("dp")
    member = lax.axis_index("group")
    owned = (event, lidar, frame)
    own_ids = lax.dynamic_slice_in_dim(sample_ids, here * rows, rows, 1)
    blocked = sample_ids.reshape(3, ranks, rows)
    far_ids = lax.dynamic_slice_in_dim(blocked, member * quarter, quarter, 2).reshape(
        3, ranks * quarter
    )
    shares = tuple((lax.dynamic_slice_in_dim(m, member * quarter, quarter, 0) for m in owned))
    zero = jnp.zeros((rows, width), jnp.float32)
    totals = (zero, zero, zero)
    pieces = (
        lax.all_gather(shares[0], "dp", axis=0, tiled=True),
        lax.all_gather(shares[1], "dp", axis=0, tiled=True),
        lax.all_gather(shares[2], "dp", axis=0, tiled=True),
    )
    updated = []
    for first in range(3):
        acc = totals[first]
        for second in range(3):
            if second != first:
                slot = first + second - 1
                coef = coefs(
                    owned[first],
                    pieces[second],
                    own_ids[first],
                    far_ids[second],
                    logit_scale[slot],
                    logit_bias[slot],
                )
                acc = acc + logit_scale[slot] * jnp.dot(
                    coef, pieces[second], preferred_element_type=jnp.float32
                )
        updated.append(acc)
    g_event = updated[0]
    g_lidar = updated[1]
    g_frame = updated[2]
    return lax.psum((g_event, g_lidar, g_frame), "group")


def solution(mesh):
    placed = (P("dp", None), P("dp", None), P("dp", None), P(), P(), P())
    return jax.shard_map(
        body,
        mesh=mesh,
        in_specs=placed,
        out_specs=(P("dp", None), P("dp", None), P("dp", None)),
        check_vma=False,
    )
```

profile of v0, /device:TPU:1, one launch (start us, length us, event | category | flops | bytes accessed | tf_op | source)
XLA Modules:
  0.0 1040.0 jit_solution(5436349587167586194)
XLA Ops:
  7.2 0.0 all-gather.6.cloned.1.call-start
  7.2 1.6 constant_dynamic-slice_fusion.3
  8.8 0.0 all-gather.6.cloned.1.call-update
  8.8 0.0 all-gather.4.cloned.1.call-start
  8.9 1.5 constant_dynamic-slice_fusion.6
  10.4 0.0 all-gather.4.cloned.1.call-update
  10.5 0.0 all-gather.8.cloned.1.call-start
  10.5 0.7 constant_dynamic-slice_fusion.2
  11.2 0.0 all-gather.8.cloned.1.call-update
  11.2 0.0 all-reduce.3.cloned.1.call-start
  11.3 1.1 reshape.19
  12.3 0.1 constant_dynamic-slice_fusion.4
  12.4 0.1 eq.41
  12.5 0.1 eq.38
  12.6 0.1 eq.88
  12.6 0.9 fusion.57
  13.5 1.4 fusion.59
  14.9 1.4 fusion.58
  16.3 264.7 %all-gather.6.cloned.1.call-done = bf16[3072,1024]{1,0:T(8,128)(2,1)} async-done(((bf16[48,1024]{1,0:T(8,128)(2,1)}), bf16[3072,1024]{1,0:T(8,128)(2,1)}) %all-gather.6.cloned.1.call-update) | async-done | bytes 6291472 | tf_op jit(solution)/shard_map/all_gather | solution.py:33
  281.1 12.3 %convolution_multiply_fusion.10 = f32[192,1024]{1,0:T(8,128)} fusion(bf16[3072,1024]{1,0:T(8,128)(2,1)} %all-gather.6.cloned.1.call-done, bf16[192,1024]{1,0:T(8,128)(2,1)S(1)} %copy-done, f32[]{:T(128)} %bitcast.5, f32[]{:T(128)} %bitcast.4, s32[192]{0:T(256)S(1)} %bitcast.79, s32[3072]{0:T(1024)S(1)} %eq.41), kind=kOutput, calls=%fused_computation.58 | convolution fusion | flops 2421424128 | bytes 7484168 | tf_op jit(solution)/shard_map/dot_general | solution.py:49
  293.3 11.5 %convolution_multiply_fusion.8 = f32[192,1024]{1,0:T(8,128)S(1)} fusion(bf16[3072,1024]{1,0:T(8,128)(2,1)} %all-gather.6.cloned.1.call-done, bf16[192,1024]{1,0:T(8,128)(2,1)S(1)} %copy-done.2, f32[]{:T(128)} %bitcast.10, f32[]{:T(128)} %bitcast.9, s32[192]{0:T(256)S(1)} %bitcast.77, s32[3072]{0:T(1024)S(1)} %eq.41), kind=kOutput, calls=%fused_computation.56 | convolution fusion | flops 2421424128 | bytes 7484168 | tf_op jit(solution)/shard_map/dot_general | solution.py:49
  304.8 283.9 %all-gather.4.cloned.1.call-done = bf16[3072,1024]{1,0:T(8,128)(2,1)} async-done(((bf16[48,1024]{1,0:T(8,128)(2,1)}), bf16[3072,1024]{1,0:T(8,128)(2,1)}) %all-gather.4.cloned.1.call-update) | async-done | bytes 6291472 | tf_op jit(solution)/shard_map/all_gather | solution.py:32
  588.7 11.5 %convolution_multiply_fusion.6 = f32[192,1024]{1,0:T(8,128)S(1)} fusion(bf16[3072,1024]{1,0:T(8,128)(2,1)} %all-gather.4.cloned.1.call-done, bf16[192,1024]{1,0:T(8,128)(2,1)S(1)} %copy-done.3, s32[192]{0:T(256)S(1)} %bitcast.75, f32[]{:T(128)} %bitcast.10, f32[]{:T(128)} %bitcast.9, s32[3072]{0:T(1024)S(1)} %eq.38), kind=kOutput, calls=%fused_computation.54 | convolution fusion | flops 2421424128 | bytes 7484168 | tf_op jit(solution)/shard_map/dot_general | solution.py:49
  600.2 12.6 %fusion.48 = f32[192,1024]{1,0:T(8,128)} fusion(f32[192,1024]{1,0:T(8,128)} %convolution_multiply_fusion.10, bf16[3072,1024]{1,0:T(8,128)(2,1)} %all-gather.4.cloned.1.call-done, bf16[192,1024]{1,0:T(8,128)(2,1)S(1)} %copy-done, s32[192]{0:T(256)S(1)} %bitcast.80, f32[]{:T(128)} %bitcast.1, f32[]{:T(128)} %bitcast, s32[3072]{0:T(1024)S(1)} %eq.38), kind=kOutput, calls=%fused_computation.60 | convolution fusion | flops 2421620736 | bytes 8270600 | tf_op jit(solution)/shard_map/dot_general | solution.py:49
  612.7 283.6 %all-gather.8.cloned.1.call-done = bf16[3072,1024]{1,0:T(8,128)(2,1)} async-done(((bf16[48,1024]{1,0:T(8,128)(2,1)}), bf16[3072,1024]{1,0:T(8,128)(2,1)}) %all-gather.8.cloned.1.call-update) | async-done | bytes 6291472 | tf_op jit(solution)/shard_map/all_gather | solution.py:31
  896.4 12.4 %fusion.49 = f32[192,1024]{1,0:T(8,128)} fusion(f32[192,1024]{1,0:T(8,128)S(1)} %convolution_multiply_fusion.8, bf16[3072,1024]{1,0:T(8,128)(2,1)} %all-gather.8.cloned.1.call-done, bf16[192,1024]{1,0:T(8,128)(2,1)S(1)} %copy-done.2, s32[192]{0:T(256)S(1)} %bitcast.78, f32[]{:T(128)} %bitcast.1, f32[]{:T(128)} %bitcast, s32[3072]{0:T(1024)S(1)} %eq.88), kind=kOutput, calls=%fused_computation.61 | convolution fusion | flops 2421620736 | bytes 8270600 | tf_op jit(solution)/shard_map/dot_general | solution.py:49
  908.7 12.0 %fusion.50 = f32[192,1024]{1,0:T(8,128)} fusion(f32[192,1024]{1,0:T(8,128)S(1)} %convolution_multiply_fusion.6, bf16[3072,1024]{1,0:T(8,128)(2,1)} %all-gather.8.cloned.1.call-done, bf16[192,1024]{1,0:T(8,128)(2,1)S(1)} %copy-done.3, s32[192]{0:T(256)S(1)} %bitcast.76, f32[]{:T(128)} %bitcast.5, f32[]{:T(128)} %bitcast.4, s32[3072]{0:T(1024)S(1)} %eq.88), kind=kOutput, calls=%fused_computation.62 | convolution fusion | flops 2421620736 | bytes 8270600 | tf_op jit(solution)/shard_map/dot_general | solution.py:49
  920.7 0.0 all-reduce.3.cloned.1.call-update
  920.7 107.5 %all-reduce.3.cloned.1.call-done = (f32[192,1024]{1,0:T(8,128)}, f32[192,1024]{1,0:T(8,128)}, f32[192,1024]{1,0:T(8,128)}) async-done(((f32[192,1024]{1,0:T(8,128)}, f32[192,1024]{1,0:T(8,128)}, f32[192,1024]{1,0:T(8,128)}), (f32[192,1024]{1,0:T(8,128)}, f32[192,1024]{1,0:T(8,128)}, f32[192,1024]{1,0:T(8,128)})) %all-reduce.3.cloned.1.call-update) | async-done | bytes 2359312 | tf_op jit(solution)/shard_map/psum | solution.py:56
  1028.3 2.2 copy.12
  1030.5 2.1 copy.13
  1032.5 0.9 copy.14
  (8 shorter events, 0.0 us)
Async XLA Ops:
  7.2 3.3 copy-start
  7.2 273.9 %all-gather.6.cloned.1.call-start = ((), (), s32[]{:S(2)}) async-start(), calls=%async_computation.1 | async-start | bytes 6389760 | tf_op jit(solution)/shard_map/all_gather | solution.py:33
  8.8 579.9 %all-gather.4.cloned.1.call-start = ((), (), s32[]{:S(2)}) async-start(), calls=%async_computation | async-start | bytes 6389760 | tf_op jit(solution)/shard_map/all_gather | solution.py:32
  10.5 885.9 %all-gather.8.cloned.1.call-start = ((), (), s32[]{:S(2)}) async-start(), calls=%async_computation.2 | async-start | bytes 6389760 | tf_op jit(solution)/shard_map/all_gather | solution.py:31
  11.2 1017.1 %all-reduce.3.cloned.1.call-start = ((), (), s32[]{:S(2)}) async-start(), calls=%async_computation.3 | async-start | bytes 4718592 | tf_op jit(solution)/shard_map/psum | solution.py:56
  281.1 12.3 %copy-start.2 = (bf16[192,1024]{1,0:T(8,128)(2,1)S(1)}, bf16[192,1024]{1,0:T(8,128)(2,1)}, u32[]{:S(2)}) copy-start(bf16[192,1024]{1,0:T(8,128)(2,1)} %param.7) | copy-start | bytes 1179652
  293.3 295.4 %copy-start.3 = (bf16[192,1024]{1,0:T(8,128)(2,1)S(1)}, bf16[192,1024]{1,0:T(8,128)(2,1)}, u32[]{:S(2)}) copy-start(bf16[192,1024]{1,0:T(8,128)(2,1)} %param.8) | copy-start | bytes 1179652
  1028.3 4.3 copy-start.1
Sparse Core Ops, SparseCore 0:
  10.4 270.6 all-gather.5
  283.4 305.2 all-gather.3
  591.1 305.2 all-gather.7
  920.9 107.3 all-reduce.2
where the time goes:
time: 1040 us
  waiting for transfers between devices  940 us (90%)
  matrix products  72.1 us (7%)
  local copies, waits for them, and re-layouts  14 us (1%)
  between operations  13.8 us (1%)
    all_gather x1, waiting for transfers between devices, body(): lax.all_gather(shares[1], 'dp', axis=0, tiled=True)  284 us
    all_gather x1, waiting for transfers between devices, body(): lax.all_gather(shares[0], 'dp', axis=0, tiled=True)  284 us
    all_gather x1, waiting for transfers between devices, body(): lax.all_gather(shares[2], 'dp', axis=0, tiled=True)  265 us
    psum x1, waiting for transfers between devices, body(): return lax.psum((g_event, g_lidar, g_frame), 'group')  108 us
    dot_general x6, matrix products, body(): jnp.dot(coef, pieces[second], preferred_element_type=jnp.float32)  72.1 us
  transfers between devices with their start and end apart: 4, of which 4 were waited for; matrix products, arithmetic and copies ran while one was open for 5% of the time, Pallas kernels for 0%

commit v1 on v0

v1 whole, which is shorter than its diff:
```python
import functools

import jax
import jax.numpy as jnp
from jax import lax
from jax.experimental import pallas as pl
from jax.experimental.pallas import tpu as pltpu
from jax.sharding import PartitionSpec as P

MESH = pl.DeviceIdType.MESH
ROWS = 192
HALF = 96
WIDTH = 1024
BLOCK = 768


class Place:
    def __init__(self):
        dp, group = lax.axis_index("dp"), lax.axis_index("group")
        self.xl, self.y, self.z = dp // 32, (dp // 8) % 4, dp % 8
        self.xh, self.c = group // 2, group % 2
        self.s = jnp.where(self.xl == 0, self.y, 7 - self.y)
        self.delta_c = (self.z + self.c + self.xh) % 2
        self.delta_a = (self.s + self.xh) % 2
        self.straight = self.c == self.xl

    def at(self, xh=None, xl=None, y=None, z=None, c=None):
        xh, xl = self.xh if xh is None else xh, self.xl if xl is None else xl
        y, z = self.y if y is None else y, self.z if z is None else z
        c = self.c if c is None else c
        return (xl * 32 + y * 8 + z, xh * 2 + c)

    def column(self, step):
        return self.at(z=(self.z + step + 8) % 8)

    def diagonal(self, step):
        s = (self.s + step + 8) % 8
        return self.at(
            xl=s // 4, y=jnp.where(s < 4, s, 7 - s), z=(self.z + step + 8) % 8
        )

    def across(self, step, y):
        x = (self.xh * 2 + self.xl + step + 4) % 4
        return self.at(xh=x // 2, xl=x % 2, y=y, c=1 - self.c)

    def other_core(self):
        return self.at(c=1 - self.c)

    def twin(self):
        return self.at(xh=1 - self.xh)


def remote(src, dst, send, recv, device):
    return pltpu.make_async_remote_copy(
        src_ref=src,
        dst_ref=dst,
        send_sem=send,
        recv_sem=recv,
        device_id=device,
        device_id_type=MESH,
    )


def signal(sem, device):
    pl.semaphore_signal(sem, inc=1, device_id=device, device_id_type=MESH)


def greet(at, twin, back):
    barrier = pltpu.get_barrier_semaphore()
    for step in (-1, 1):
        signal(barrier, at.column(step))
        signal(barrier, at.diagonal(step))
    signal(barrier, at.other_core())
    if twin:
        signal(barrier, at.twin())

    @pl.when(at.straight)
    def _():
        for step in range(1, 4):
            signal(barrier, at.at(y=(at.y + step) % 4))

    @pl.when(jnp.logical_not(at.straight))
    def _():
        for y in range(4):
            signal(barrier, at.across(1 if back else -1, y))

    pl.semaphore_wait(barrier, 5 + int(twin) + jnp.where(at.straight, 3, 4))


class RingGather:
    def __init__(self, place, delta, neighbour, far, own, slot, send, recv):
        self.place, self.delta, self.neighbour, self.far = place, delta, neighbour, far
        self.own, self.slot, self.send, self.recv = own, slot, send, recv

    def copy(self, direction, message, source, src=None):
        d = 0 if direction == self.far else 1
        dst = self.slot((source + 8) % 8)
        return remote(
            dst if src is None else src,
            dst,
            self.send.at[d, message],
            self.recv.at[d, message],
            self.neighbour(direction),
        )

    def start(self):
        @pl.when(self.delta == 0)
        def _():
            for direction in (self.far, -self.far):
                self.copy(direction, 0, self.place, self.own).start()

    def stage(self, st, arrived=None):
        message = (st - 1) // 2
        odd = st % 2

        @pl.when(self.delta == odd)
        def _():
            for direction in (self.far, -self.far):
                if direction != self.far and st > 3:
                    continue
                source = self.place - direction * st
                self.copy(direction, message, source).wait_recv()
                if st < (4 if direction == self.far else 3):
                    self.copy(direction, message + 1 - odd, source).start()
                if arrived is not None:
                    arrived((source + 8) % 8)

    def finish(self):
        for direction in (self.far, -self.far):
            for message in range(2):
                if direction != self.far and message == 1:

                    @pl.when(self.delta == 0)
                    def _():
                        self.copy(direction, 1, self.place).wait_send()

                else:
                    self.copy(direction, message, self.place).wait_send()


def gather_kernel(
    a_own, b_own, c_own, a_all, b_all, c_all,
    c_send, c_recv, a_send, a_recv, t_send, t_recv, b_send, b_recv, own_sem,
):
    at = Place()
    half = pl.ds(at.c * HALF, HALF)
    ring_c = RingGather(
        at.z, at.delta_c, at.column, 1, c_own, lambda q: c_all.at[q // 2], c_send, c_recv
    )
    ring_a = RingGather(
        at.s, at.delta_a, at.diagonal, -1, a_own.at[half], lambda q: a_all.at[q // 2, half], a_send, a_recv
    )
    own_c = pltpu.make_async_copy(c_own, c_all.at[at.z // 2], own_sem.at[0])
    own_a = pltpu.make_async_copy(a_own, a_all.at[at.s // 2], own_sem.at[1])
    own_b = pltpu.make_async_copy(b_own, b_all.at[at.y], own_sem.at[2])

    def pass_over(q):
        view = a_all.at[q // 2, half]
        return remote(view, view, t_send.at[q // 2], t_recv.at[q // 2], at.other_core())

    def taken_over(q):
        view = a_all.at[q // 2, pl.ds((1 - at.c) * HALF, HALF)]
        return remote(view, view, t_send.at[q // 2], t_recv.at[q // 2], at.other_core())

    def straight_copy(step):
        return remote(
            b_own, b_all.at[at.y], b_send.at[step], b_recv.at[at.y], at.at(y=(at.y + step) % 4)
        )

    def across_copy(y):
        return remote(
            b_own, b_all.at[at.y], b_send.at[y], b_recv.at[at.y], at.across(1, y)
        )

    def b_arrival(y):
        return remote(
            b_own, b_all.at[y], b_send.at[0], b_recv.at[y], at.other_core()
        )

    greet(at, twin=False, back=False)
    ring_c.start()
    ring_a.start()

    @pl.when(at.delta_c == 0)
    def _():
        own_c.start()

    @pl.when(at.delta_a == 0)
    def _():
        own_a.start()

    @pl.when(at.straight)
    def _():
        own_b.start()
        for step in range(1, 4):
            straight_copy(step).start()

    @pl.when(jnp.logical_not(at.straight))
    def _():
        for y in range(4):
            across_copy(y).start()

    for st in range(1, 5):
        ring_c.stage(st)
        ring_a.stage(st, lambda q: pass_over(q).start())
    ring_c.finish()
    ring_a.finish()

    @pl.when(at.delta_c == 0)
    def _():
        own_c.wait()

    @pl.when(at.delta_a == 0)
    def _():
        own_a.wait()

    @pl.when(at.straight)
    def _():
        own_b.wait()
        for step in range(1, 4):
            straight_copy(step).wait_send()
            b_arrival((at.y + step) % 4).wait_recv()

    @pl.when(jnp.logical_not(at.straight))
    def _():
        for y in range(4):
            across_copy(y).wait_send()
            b_arrival(y).wait_recv()

    for slot in range(4):

        @pl.when(jnp.logical_or(at.delta_a == 1, at.s // 2 != slot))
        def _():
            pass_over(2 * slot).wait_send()
            taken_over(2 * slot).wait_recv()


def gather(a, b, c):
    whole = jax.ShapeDtypeStruct((4, ROWS, WIDTH), jnp.bfloat16)
    hbm = pl.BlockSpec(memory_space=pl.ANY)
    dma = pltpu.SemaphoreType.DMA
    return pl.pallas_call(
        gather_kernel,
        out_shape=(whole, whole, whole),
        in_specs=[hbm] * 3,
        out_specs=(hbm, hbm, hbm),
        scratch_shapes=[
            dma((2, 2)), dma((2, 2)), dma((2, 2)), dma((2, 2)),
            dma((4,)), dma((4,)), dma((4,)), dma((4,)), dma((3,)),
        ],
        compiler_params=pltpu.CompilerParams(collective_id=0, has_side_effects=True),
    )(a, b, c)


TILE = 256


def compute_kernel(
    scale, bias, a_col, b_col, b_row, c_row, a, b, c, ga, gb, gc, coef
):
    def pair(left, right, left_ids, right_ids, p, g_left, g_right, new_left, new_right):
        def rows(i, _):
            span = pl.ds(pl.multiple_of(i * TILE, TILE), TILE)
            logits = lax.dot_general(
                left[span, :], right[...], (((1,), (1,)), ((), ())),
                preferred_element_type=jnp.float32,
            )
            u = scale[p] * logits + bias[p]
            label = (left_ids[span, :] == right_ids[...]).astype(jnp.float32)
            tile = (jax.nn.sigmoid(u) - label).astype(jnp.bfloat16)
            coef[span, :] = tile
            part = scale[p] * jnp.dot(
                tile, right[...], preferred_element_type=jnp.float32
            )
            g_left[span, :] = part if new_left else g_left[span, :] + part
            return 0

        lax.fori_loop(0, BLOCK // TILE, rows, 0)
        for i in range(BLOCK // TILE):
            span = pl.ds(i * TILE, TILE)
            part = scale[p] * lax.dot_general(
                coef[:, span], left[...], (((0,), (0,)), ((), ())),
                preferred_element_type=jnp.float32,
            )
            g_right[span, :] = part if new_right else g_right[span, :] + part

    pair(b, c, b_col, c_row, 2, gb, gc, True, True)
    pair(a, b, a_col, b_row, 0, ga, gb, True, False)
    pair(a, c, a_col, c_row, 1, ga, gc, False, False)


def compute(scale, bias, a_ids, b_ids, c_ids, a, b, c):
    vmem = pl.BlockSpec(memory_space=pltpu.VMEM)
    smem = pl.BlockSpec(memory_space=pltpu.SMEM)
    part = jax.ShapeDtypeStruct((BLOCK, WIDTH), jnp.float32)
    return pl.pallas_call(
        compute_kernel,
        out_shape=(part, part, part),
        in_specs=[smem, smem] + [vmem] * 7,
        out_specs=(vmem, vmem, vmem),
        scratch_shapes=[pltpu.VMEM((BLOCK, BLOCK), jnp.bfloat16)],
        compiler_params=pltpu.CompilerParams(vmem_limit_bytes=56 << 20),
    )(
        scale, bias, a_ids.reshape(BLOCK, 1), b_ids.reshape(BLOCK, 1),
        b_ids.reshape(1, BLOCK), c_ids.reshape(1, BLOCK), a, b, c,
    )


class RingReduce:
    def __init__(self, place, delta, neighbour, far, part, box, send, recv):
        self.place, self.delta, self.neighbour, self.far = place, delta, neighbour, far
        self.part, self.box, self.send, self.recv = part, box, send, recv

    def copy(self, direction, message, dest, src=None):
        d = 0 if direction == self.far else 1
        return remote(
            self.part((dest + 8) % 8) if src is None else src,
            self.box.at[d, message],
            self.send.at[d, message],
            self.recv.at[d, message],
            self.neighbour(direction),
        )

    def stage(self, st):
        odd = (st - 1) % 2

        @pl.when(self.delta == odd)
        def _():
            for direction in (self.far, -self.far):
                first = 1 if direction == self.far else 2
                if st < first:
                    continue
                d = 0 if direction == self.far else 1
                dest = self.place + direction * (5 - st)
                src = None
                if st > first:
                    message = (st - 2) // 2
                    self.copy(direction, message, dest).wait_recv()
                    src = self.box.at[d, message]
                    src[...] = src[...] + self.part((dest + 8) % 8)[...]
                self.copy(direction, (st - 1) // 2, dest, src).start()

    def last(self, out):
        @pl.when(self.delta == 0)
        def _():
            for direction in (self.far, -self.far):
                self.copy(direction, 1, self.place).wait_recv()
            out[...] = self.part(self.place)[...] + (self.box[0, 1] + self.box[1, 1])

    def finish(self):
        for direction in (self.far, -self.far):
            for message in range(2):
                first = 1 if direction == self.far else 2
                for odd in range(2):
                    stages = [
                        st for st in range(first, 5)
                        if (st - 1) % 2 == odd and (st - 1) // 2 == message
                    ]
                    if stages:

                        @pl.when(self.delta == odd)
                        def _():
                            self.copy(direction, message, self.place).wait_send()


def reduce_kernel(
    a_in, b_in, c_in, a_out, b_out, c_out,
    a_box, a_near, b_box, c_box, b_sum, c_sum, near_box, twin_box,
    c_send, c_recv, a_send, a_recv, n_send, n_recv, b_send, b_recv, f_send, f_recv,
):
    at = Place()
    mine = pl.ds(at.c * HALF, HALF)
    theirs = pl.ds((1 - at.c) * HALF, HALF)
    ring_c = RingReduce(
        at.z, at.delta_c, at.column, 1, lambda q: c_in.at[q // 2], c_box, c_send, c_recv
    )
    ring_a = RingReduce(
        at.s, at.delta_a, at.diagonal, -1, lambda q: a_near.at[q // 2], a_box, a_send, a_recv
    )
    near = remote(
        a_in.at[:, theirs], a_near, n_send.at[0], n_recv.at[0], at.other_core()
    )

    def straight_copy(step):
        y = (at.y + step) % 4
        return remote(
            b_in.at[y], b_box.at[at.y], b_send.at[step], b_recv.at[at.y], at.at(y=y)
        )

    def across_copy(y):
        return remote(
            b_in.at[y], b_box.at[at.y], b_send.at[y], b_recv.at[at.y], at.across(-1, y)
        )

    def b_arrival(y):
        return remote(b_in.at[y], b_box.at[y], b_send.at[0], b_recv.at[y], at.other_core())

    greet(at, twin=True, back=True)
    near.start()

    @pl.when(at.straight)
    def _():
        for step in range(1, 4):
            straight_copy(step).start()

    @pl.when(jnp.logical_not(at.straight))
    def _():
        for y in range(4):
            across_copy(y).start()

    ring_c.stage(1)
    near.wait()
    for slot in range(4):
        a_near[slot] = a_near[slot] + a_in[slot, mine, :]
    ring_a.stage(1)
    for st in range(2, 5):
        ring_c.stage(st)
        ring_a.stage(st)
    ring_c.last(c_sum)
    ring_a.last(a_out.at[mine])

    @pl.when(at.straight)
    def _():
        b_sum[...] = b_in[at.y]
        for step in range(1, 4):
            straight_copy(step).wait_send()
            b_arrival((at.y + step) % 4).wait_recv()
            b_sum[...] = b_sum[...] + b_box[(at.y + step) % 4]

    @pl.when(jnp.logical_not(at.straight))
    def _():
        for y in range(4):
            across_copy(y).wait_send()
            b_arrival(y).wait_recv()
        b_sum[...] = (b_box[0] + b_box[1]) + (b_box[2] + b_box[3])

    ring_c.finish()
    ring_a.finish()

    near_b = remote(b_sum.at[theirs], near_box.at[0], f_send.at[0], f_recv.at[0], at.other_core())
    near_c = remote(c_sum.at[theirs], near_box.at[1], f_send.at[1], f_recv.at[1], at.other_core())
    near_b.start()

    @pl.when(at.delta_c == 0)
    def _():
        near_c.start()
        c_out[mine, :] = c_sum[mine, :]

    @pl.when(at.delta_c == 1)
    def _():
        near_c.wait_recv()
        c_out[mine, :] = near_box[1]

    near_b.wait()
    b_out[mine, :] = b_sum[mine, :] + near_box[0]

    far_b = remote(b_out.at[mine], twin_box.at[0], f_send.at[2], f_recv.at[2], at.twin())
    far_c = remote(c_out.at[mine], twin_box.at[1], f_send.at[3], f_recv.at[3], at.twin())
    far_a = remote(a_out.at[mine], a_out.at[mine], f_send.at[4], f_recv.at[4], at.twin())
    far_b.start()
    far_c.start()

    @pl.when(at.delta_a == 0)
    def _():
        far_a.start()

    @pl.when(at.delta_c == 0)
    def _():
        near_c.wait_send()

    def last(ref, i):
        return remote(ref.at[mine], ref.at[mine], f_send.at[i], f_recv.at[i], at.other_core())

    def last_arrival(ref, i):
        return remote(ref.at[theirs], ref.at[theirs], f_send.at[i], f_recv.at[i], at.other_core())

    far_b.wait()
    b_out[mine, :] = b_out[mine, :] + twin_box[0]
    last(b_out, 5).start()
    far_c.wait()
    c_out[mine, :] = c_out[mine, :] + twin_box[1]
    last(c_out, 6).start()

    @pl.when(at.delta_a == 0)
    def _():
        far_a.wait_send()

    @pl.when(at.delta_a == 1)
    def _():
        far_a.wait_recv()

    last(a_out, 7).start()
    for i, ref in ((5, b_out), (6, c_out), (7, a_out)):
        last(ref, i).wait_send()
        last_arrival(ref, i).wait_recv()


def reduce(a, b, c):
    vmem = pl.BlockSpec(memory_space=pltpu.VMEM)
    out = jax.ShapeDtypeStruct((ROWS, WIDTH), jnp.float32)
    dma = pltpu.SemaphoreType.DMA
    f32 = jnp.float32
    return pl.pallas_call(
        reduce_kernel,
        out_shape=(out, out, out),
        in_specs=[vmem] * 3,
        out_specs=(vmem, vmem, vmem),
        scratch_shapes=[
            pltpu.VMEM((2, 2, HALF, WIDTH), f32),
            pltpu.VMEM((4, HALF, WIDTH), f32),
            pltpu.VMEM((4, ROWS, WIDTH), f32),
            pltpu.VMEM((2, 2, ROWS, WIDTH), f32),
            pltpu.VMEM((ROWS, WIDTH), f32),
            pltpu.VMEM((ROWS, WIDTH), f32),
            pltpu.VMEM((2, HALF, WIDTH), f32),
            pltpu.VMEM((2, HALF, WIDTH), f32),
            dma((2, 2)), dma((2, 2)), dma((2, 2)), dma((2, 2)),
            dma((1,)), dma((1,)), dma((4,)), dma((4,)), dma((8,)), dma((8,)),
        ],
        compiler_params=pltpu.CompilerParams(
            collective_id=1, has_side_effects=True, vmem_limit_bytes=56 << 20
        ),
    )(a, b, c)


def body(event, lidar, frame, sample_ids, logit_scale, logit_bias):
    at = Place()
    blocked = sample_ids.reshape(3, 64, ROWS)

    def ids(which, shards):
        return jnp.concatenate(
            [lax.dynamic_slice(blocked, (which, d, 0), (1, 1, ROWS)).reshape(ROWS) for d in shards]
        )

    first = (at.z - at.s + 8) % 8
    a_shards = []
    for slot in range(4):
        s = 2 * slot + at.xh
        y = jnp.where(s < 4, s, 7 - s)
        a_shards.append((s // 4) * 32 + y * 8 + (first + s) % 8)
    b_shards = [at.c * 32 + y * 8 + at.z for y in range(4)]
    parity = (at.c + at.xh) % 2
    c_shards = [at.xl * 32 + at.y * 8 + 2 * slot + parity for slot in range(4)]

    a, b, c = (m.reshape(BLOCK, WIDTH) for m in gather(event, lidar, frame))
    parts = compute(
        logit_scale, logit_bias, ids(0, a_shards), ids(1, b_shards), ids(2, c_shards), a, b, c
    )
    return reduce(*(g.reshape(4, ROWS, WIDTH) for g in parts))


def solution(mesh):
    placed = (P("dp", None), P("dp", None), P("dp", None), P(), P(), P())
    return jax.shard_map(
        body,
        mesh=mesh,
        in_specs=placed,
        out_specs=(P("dp", None), P("dp", None), P("dp", None)),
        check_vma=False,
    )
```

time: 1040 us -> 190 us (0.18)
  waiting for transfers between devices: 940 us -> 0 us
  Pallas kernels: 0 us -> 179 us
  matrix products: 72.1 us -> 0 us
  between operations: 13.8 us -> 1 us
    all_gather x3 -> x0, waiting for transfers between devices: 832 us -> none  [the longest x1 284 us: body(): lax.all_gather(shares[1], 'dp', axis=0, tiled=True)]
    pallas_call x0 -> x3, Pallas kernels: none -> 179 us  [the longest x1 116 us: reduce(): pl.pallas_call(reduce_kernel, out_shape=(out, out, out), in_specs=[vmem]...]
    psum x1 -> x0, waiting for transfers between devices: 108 us -> none  [body(): return lax.psum((g_event, g_lidar, g_frame), 'group')]
    dot_general x6 -> x0, matrix products: 72.1 us -> none  [body(): jnp.dot(coef, pieces[second], preferred_element_type=jnp.float32)]
  transfers between devices with their start and end apart: 4 -> 0, of which waited for: 4 -> 0; matrix products, arithmetic and copies ran while one was open for 5% -> 0% of each run, Pallas kernels for 0% -> 0%
where the time goes in v1:
time: 190 us
  Pallas kernels  179 us (94%)
  local copies, waits for them, and re-layouts  9.23 us (5%)
    pallas_call x1, Pallas kernels, reduce(): pl.pallas_call(reduce_kernel, out_shape=(out, out, out), in_specs=[vmem]...  116 us
    pallas_call x1, Pallas kernels, gather(): pl.pallas_call(gather_kernel, out_shape=(whole, whole, whole), in_specs=[...  42.6 us
    pallas_call x1, Pallas kernels, compute(): pl.pallas_call(compute_kernel, out_shape=(part, part, part), in_specs=[sm...  20.8 us
    unnamed x5, local copies, waits for them, and re-layouts  5.13 us

profile of v1, /device:TPU:1, one launch (start us, length us, event | category | flops | bytes accessed | tf_op | source)
XLA Modules:
  0.0 189.8 jit_solution(13205797843093898633)
XLA Ops:
  1.0 1.1 reshape.75
  2.1 0.1 pad_add_fusion.2
  2.2 0.6 reshape.91.c_row
  2.7 0.1 pad_add_fusion.1
  2.8 0.6 reshape.86.b_row
  3.4 0.1 pad_add_fusion
  3.5 0.9 reshape.98.a_col
  4.4 0.9 reshape.99.b_col
  5.3 42.6 %shard_map.85 = (bf16[4,192,1024]{2,1,0:T(8,128)(2,1)}, bf16[4,192,1024]{2,1,0:T(8,128)(2,1)}, bf16[4,192,1024]{2,1,0:T(8,128)(2,1)}) custom-call(bf16[192,1024]{1,0:T(8,128)(2,1)} %a_own.1, bf16[192,1024]{1,0:T(8,128)(2,1)} %b_own.1, bf16[192,1024]{1,0:T(8,128)(2,1)} %c_own.1), custom_call_target="tpu_custom_call" | custom-call | tf_op jit(solution)/shard_map/pallas_call | solution.py:242
  47.9 20.8 %shard_map.86 = (f32[768,1024]{1,0:T(8,128)}, f32[768,1024]{1,0:T(8,128)}, f32[768,1024]{1,0:T(8,128)}) custom-call(f32[3]{0:T(128)} %scale.1, f32[3]{0:T(128)} %bias.1, s32[768,1]{1,0:T(8,128)} %reshape.98.a_col, s32[768,1]{1,0:T(8,128)} %reshape.99.b_col, s32[1,768]{1,0:T(1,128)} %reshape.86.b_row, s32[1,768]{1,0:T(1,128)} %reshape.91.c_row, ...), custom_call_target="tpu_custom_call" | custom-call | tf_op jit(solution)/shard_map/pallas_call | solution.py:296
  68.7 116.0 %shard_map.87 = (f32[192,1024]{1,0:T(8,128)}, f32[192,1024]{1,0:T(8,128)}, f32[192,1024]{1,0:T(8,128)}) custom-call(f32[4,192,1024]{2,1,0:T(8,128)} %bitcast.18, f32[4,192,1024]{2,1,0:T(8,128)} %bitcast.19, f32[4,192,1024]{2,1,0:T(8,128)} %bitcast.20), custom_call_target="tpu_custom_call" | custom-call | tf_op jit(solution)/shard_map/pallas_call | solution.py:503
  184.7 0.0 copy-start
  184.7 2.2 %copy.14 = f32[192,1024]{1,0:T(8,128)} copy(f32[192,1024]{1,0:T(8,128)} %get-tuple-element.30) | data formatting | bytes 1572864
  186.9 2.1 %copy.15 = f32[192,1024]{1,0:T(8,128)} copy(f32[192,1024]{1,0:T(8,128)} %get-tuple-element.31) | data formatting | bytes 1572864
  189.0 0.0 copy-done
  189.0 0.9 copy.16
  (1 shorter events, 0.0 us)
Async XLA Ops:
  184.7 4.3 %copy-start = (f32[192,1024]{1,0:T(8,128)S(1)}, f32[192,1024]{1,0:T(8,128)}, u32[]{:S(2)}) copy-start(f32[192,1024]{1,0:T(8,128)} %get-tuple-element.32) | copy-start | bytes 2359300

commit v2 on v0

v2 whole, which is shorter than its diff:
```python
import math

import jax
import jax.numpy as jnp
from jax import lax
from jax.experimental import pallas as pl
from jax.experimental.pallas import tpu as pltpu
from jax.sharding import PartitionSpec as P

MESH = pl.DeviceIdType.MESH
ROWS = 192
HALF = 96
QUARTER = 48
WIDTH = 1024
BLOCK = 768
TILE = 256
LOG2E = math.log2(math.e)
OFFSETS = {8: (4, 3, -3, 2, -2, 1, -1, 0), 4: (2, 1, -1, 0)}


class Place:
    def __init__(self):
        dp, group = lax.axis_index("dp"), lax.axis_index("group")
        self.xl, self.y, self.z = dp // 32, (dp // 8) % 4, dp % 8
        self.xh, self.c = group // 2, group % 2
        self.s = jnp.where(self.xl == 0, self.y, 7 - self.y)

    def at(self, xh=None, xl=None, y=None, z=None, c=None):
        xh, xl = self.xh if xh is None else xh, self.xl if xl is None else xl
        y, z = self.y if y is None else y, self.z if z is None else z
        c = self.c if c is None else c
        return (xl * 32 + y * 8 + z, xh * 2 + c)

    def column(self, step):
        return self.at(z=(self.z + step + 8) % 8)

    def row(self, step):
        return self.at(y=(self.y + step + 4) % 4)

    def diagonal(self, step):
        s = (self.s + step + 8) % 8
        return self.at(
            xl=s // 4, y=jnp.where(s < 4, s, 7 - s), z=(self.z + step + 8) % 8
        )

    def beside(self):
        return self.at(xl=1 - self.xl)

    def other_core(self):
        return self.at(c=1 - self.c)

    def twin(self, other=False):
        return self.at(xh=1 - self.xh, c=1 - self.c if other else self.c)


def remote(src, dst, send, recv, device):
    return pltpu.make_async_remote_copy(
        src_ref=src,
        dst_ref=dst,
        send_sem=send,
        recv_sem=recv,
        device_id=device,
        device_id_type=MESH,
    )


def slot(n, offset):
    return OFFSETS[n].index(n // 2 if offset == -(n // 2) else offset)


class RingGather:
    def __init__(self, n, neighbour, far, own, view, send, recv):
        self.n, self.neighbour, self.far, self.own = n, neighbour, far, own
        self.view, self.send, self.recv = view, send, recv

    def reach(self, direction):
        return self.n // 2 if direction == self.far else self.n // 2 - 1

    def copy(self, direction, step):
        d = 0 if direction == self.far else 1
        src = self.own if step == 1 else self.view(slot(self.n, -direction * (step - 1)))
        return remote(
            src,
            self.view(slot(self.n, -direction * step)),
            self.send.at[d, step - 1],
            self.recv.at[d, step - 1],
            self.neighbour(direction),
        )

    def start(self):
        for direction in (self.far, -self.far):
            self.copy(direction, 1).start()

    def stage(self, step, arrived=None):
        for direction in (self.far, -self.far):
            if step <= self.reach(direction):
                self.copy(direction, step).wait_recv()
                if step < self.reach(direction):
                    self.copy(direction, step + 1).start()
                if arrived is not None:
                    arrived(slot(self.n, -direction * step))

    def finish(self):
        for direction in (self.far, -self.far):
            for step in range(1, self.reach(direction) + 1):
                self.copy(direction, step).wait_send()


class Parcel:
    def __init__(self, out, out_scale, into, into_scale, send, recv, device):
        self.out, self.out_scale = out, out_scale
        self.into, self.into_scale = into, into_scale
        self.data = remote(out, into, send.at[0], recv.at[0], device)
        self.scale = remote(out_scale, into_scale, send.at[1], recv.at[1], device)

    def pack(self, value):
        top = jnp.max(jnp.abs(value), axis=0, keepdims=True)
        top = jnp.maximum(jnp.max(top, axis=1, keepdims=True), 1e-30)
        self.out[...] = (
            jnp.round(value * (32767.0 / top)).astype(jnp.int32).astype(jnp.int16)
        )
        self.out_scale[...] = jnp.broadcast_to(top * (1 / 32767.0), (8, 128))

    def start(self, value):
        self.pack(value)
        self.data.start()
        self.scale.start()

    def take(self):
        self.data.wait_recv()
        self.scale.wait_recv()
        return opened(self.into, self.into_scale)

    def sent(self):
        self.data.wait_send()
        self.scale.wait_send()


def opened(values, scale):
    return values[...].astype(jnp.int32).astype(jnp.float32) * scale[0:1, 0:1]


class RingReduce:
    def __init__(self, n, neighbour, far, part, box):
        self.n, self.neighbour, self.far, self.part, self.box = n, neighbour, far, part, box

    def parcel(self, direction, stage):
        out, out_scale, into, into_scale, send, recv = self.box
        i = stage - 1 if direction == self.far else self.n // 2 + stage - 2
        return Parcel(
            out.at[i], out_scale.at[i], into.at[i], into_scale.at[i],
            send.at[i], recv.at[i], self.neighbour(direction),
        )

    def first(self, direction):
        return 1 if direction == self.far else 2

    def stage(self, st):
        for direction in (self.far, -self.far):
            if st < self.first(direction):
                continue
            value = self.part(slot(self.n, direction * (self.n // 2 + 1 - st)))
            if st > self.first(direction):
                value = value + self.parcel(direction, st - 1).take()
            self.parcel(direction, st).start(value)

    def last(self):
        value = self.part(slot(self.n, 0))
        for direction in (self.far, -self.far):
            value = value + self.parcel(direction, self.n // 2).take()
        return value

    def finish(self):
        for direction in (self.far, -self.far):
            for st in range(self.first(direction), self.n // 2 + 1):
                self.parcel(direction, st).sent()


def greet(at):
    barrier = pltpu.get_barrier_semaphore()
    others = [at.column(-1), at.column(1), at.diagonal(-1), at.diagonal(1), at.row(-1), at.row(1)]
    others += [at.beside(), at.other_core(), at.twin(), at.twin(True)]
    for device in others:
        pl.semaphore_signal(barrier, inc=1, device_id=device, device_id_type=MESH)
    pl.semaphore_wait(barrier, len(others))


def coefficients(rows, cols, row_ids, col_ids, scale, bias):
    logits = lax.dot_general(
        rows, cols, (((1,), (1,)), ((), ())), preferred_element_type=jnp.float32
    )
    power = jnp.minimum(logits * (scale * -LOG2E) - bias * LOG2E, 126.0)
    sigmoid = 1.0 / (1.0 + jnp.exp2(power))
    label = jnp.where(row_ids == col_ids, 1.0, 0.0)
    return (sigmoid - label).astype(jnp.bfloat16)


def product(coef, rows):
    return jnp.dot(coef, rows, preferred_element_type=jnp.float32)


def product_t(coef, rows):
    return lax.dot_general(
        coef, rows, (((0,), (0,)), ((), ())), preferred_element_type=jnp.float32
    )


def kernel(
    scale, bias, a_col, a_row, b_row, c_col, a_own, b_own, c_own, a_out, b_out, c_out,
    a, b, c, ga, gb, gc, coef_ab, coef_ca, coef_cb,
    a_near, a_box, a_box_scale, b_box, b_box_scale, c_box, c_box_scale, e_box, e_box_scale, sums,
    ga_send, ga_recv, gb_send, gb_recv, gc_send, gc_recv, gt_send, gt_recv, gx_send, gx_recv, own_sem,
    ra_send, ra_recv, rb_send, rb_recv, rc_send, rc_recv, rt_send, rt_recv, re_send, re_recv, rf_send, rf_recv,
):
    at = Place()

    def span(start, size):
        return pl.ds(pl.multiple_of(start, 16), size)

    k = (at.c + at.xh) % 2
    my_b, my_c, my_a = span(at.c * HALF, HALF), span(k * HALF, HALF), span(at.xh * HALF, HALF)
    my_quarter = span(at.xh * HALF + at.c * QUARTER, QUARTER)

    def a_quarter(i, core):
        return a.at[span(i * HALF + core * QUARTER, QUARTER)]

    def piece(ref, i):
        return ref.at[i * HALF : (i + 1) * HALF]

    ring_c = RingGather(8, at.column, 1, c_own.at[my_c], lambda i: piece(c, i), gc_send, gc_recv)
    ring_a = RingGather(8, at.diagonal, -1, a_own.at[my_quarter], lambda i: a_quarter(i, at.c), ga_send, ga_recv)
    ring_b = [
        RingGather(4, at.row, 1, b_own.at[my_b], lambda i: piece(b, i), gb_send.at[0], gb_recv.at[0]),
        RingGather(4, at.row, -1, piece(b, 7), lambda i: piece(b, 4 + i), gb_send.at[1], gb_recv.at[1]),
    ]
    beside = remote(b_own.at[my_b], piece(b, 7), gx_send.at[0], gx_recv.at[0], at.beside())
    own = [
        pltpu.make_async_copy(a_own.at[my_a], piece(a, 7), own_sem.at[0]),
        pltpu.make_async_copy(b_own.at[my_b], piece(b, 3), own_sem.at[1]),
        pltpu.make_async_copy(c_own.at[my_c], piece(c, 7), own_sem.at[2]),
    ]

    def pass_over(i, core):
        view = a_quarter(i, core)
        return remote(view, view, gt_send.at[i], gt_recv.at[i], at.other_core())

    greet(at)
    ring_a.start()
    beside.start()
    ring_b[0].start()
    ring_c.start()
    for copy in own:
        copy.start()

    def to_other(i):
        pass_over(i, at.c).start()

    ring_a.stage(1, to_other)
    beside.wait_recv()
    ring_b[1].start()
    ring_c.stage(1)
    ring_a.stage(2, to_other)
    ring_b[0].stage(1)
    ring_b[1].stage(1)
    ring_a.stage(3, to_other)
    ring_c.stage(2)
    ring_b[0].stage(2)
    ring_b[1].stage(2)
    ring_a.stage(4, to_other)
    for copy in own:
        copy.wait()
    for i in range(7):
        pass_over(i, 1 - at.c).wait_recv()

    def ab_rows(i):
        rows = pl.ds(i * TILE, TILE)
        tile = coefficients(a[rows, :], b[...], a_col[rows, :], b_row[...], scale[0], bias[0])
        coef_ab[rows, :] = tile
        ga[rows, :] = scale[0] * product(tile, b[...])

    ab_rows(0)
    ring_c.stage(3)
    ab_rows(1)
    ab_rows(2)
    ring_c.stage(4)
    for i in range(BLOCK // TILE):
        cols = pl.ds(i * TILE, TILE)
        gb[cols, :] = scale[0] * product_t(coef_ab[:, cols], a[...])

    reduce_a = RingReduce(
        8, at.diagonal, -1,
        lambda i: ga[pl.ds(pl.multiple_of(i * HALF + at.c * QUARTER, 8), QUARTER), :] + a_near[i],
        (a_box.at[0], a_box_scale.at[0], a_box.at[1], a_box_scale.at[1], ra_send, ra_recv),
    )
    reduce_c = RingReduce(
        8, at.column, 1, lambda i: gc[i * HALF : (i + 1) * HALF, :],
        (c_box.at[0], c_box_scale.at[0], c_box.at[1], c_box_scale.at[1], rc_send, rc_recv),
    )
    reduce_b = [
        RingReduce(
            4, at.row, 1 - 2 * r, lambda i, r=r: gb[(4 * r + i) * HALF : (4 * r + i + 1) * HALF, :],
            (b_box.at[0, r], b_box_scale.at[0, r], b_box.at[1, r], b_box_scale.at[1, r], rb_send.at[r], rb_recv.at[r]),
        )
        for r in range(2)
    ]

    for g in range(4):
        rows = pl.ds(g * ROWS, ROWS)
        tile_a = coefficients(c[rows, :], a[...], c_col[rows, :], a_row[...], scale[1], bias[1])
        tile_b = coefficients(c[rows, :], b[...], c_col[rows, :], b_row[...], scale[2], bias[2])
        coef_ca[rows, :] = tile_a
        coef_cb[rows, :] = tile_b
        gc[rows, :] = scale[1] * product(tile_a, a[...]) + scale[2] * product(tile_b, b[...])
        reduce_c.stage(g + 1)

    def near(i, core):
        return remote(
            ga.at[pl.ds(pl.multiple_of(i * HALF + core * QUARTER, 8), QUARTER)], a_near.at[i],
            rt_send.at[i], rt_recv.at[i], at.other_core(),
        )

    for i in range(BLOCK // TILE):
        cols = pl.ds(i * TILE, TILE)
        ga[cols, :] = ga[cols, :] + scale[1] * product_t(coef_ca[:, cols], c[...])
    for i in range(8):
        near(i, 1 - at.c).start()
    for i in range(BLOCK // TILE):
        cols = pl.ds(i * TILE, TILE)
        gb[cols, :] = gb[cols, :] + scale[2] * product_t(coef_cb[:, cols], c[...])
    near(0, 1 - at.c).wait_recv()
    reduce_a.stage(1)
    for r in range(2):
        reduce_b[r].stage(1)
    for i in range(1, 8):
        near(i, 1 - at.c).wait_recv()

    out_e, out_e_scale = e_box.at[0], e_box_scale.at[0]
    in_e, in_e_scale = e_box.at[1], e_box_scale.at[1]

    def extra(i, device, rows=HALF):
        return Parcel(
            out_e.at[i, 0:rows], out_e_scale.at[i], in_e.at[i, 0:rows], in_e_scale.at[i],
            re_send.at[i], re_recv.at[i], device,
        )

    twin_c = extra(0, at.twin(True))
    beside_b = extra(1, at.beside())
    twin_b = extra(2, at.twin())
    twin_a = extra(3, at.twin(), QUARTER)

    def to_core(out, rows, i):
        return remote(out.at[rows], out.at[rows], rf_send.at[i], rf_recv.at[i], at.other_core())

    def settle(parcel, out, rows, i):
        mine = opened(parcel.out, parcel.out_scale)
        out[rows, :] = mine + parcel.take()
        to_core(out, rows, i).start()

    reduce_a.stage(2)
    for r in range(2):
        reduce_b[r].stage(2)
    twin_c.start(reduce_c.last())
    reduce_a.stage(3)
    sums[...] = reduce_b[0].last()
    beside_b.start(reduce_b[1].last())
    reduce_a.stage(4)
    settle(twin_c, c_out, my_c, 0)
    twin_b.start(sums[...] + beside_b.take())
    twin_a.start(reduce_a.last())
    a_out[my_quarter, :] = opened(twin_a.out, twin_a.out_scale)
    to_core(a_out, my_quarter, 2).start()
    settle(twin_b, b_out, my_b, 1)
    far_quarter = span((1 - at.xh) * HALF + at.c * QUARTER, QUARTER)
    a_out[far_quarter, :] = twin_a.take()
    to_core(a_out, far_quarter, 3).start()

    for ring in (ring_a, ring_c, *ring_b, reduce_a, reduce_c, *reduce_b):
        ring.finish()
    beside.wait_send()
    for i in range(7):
        pass_over(i, at.c).wait_send()
    for i in range(8):
        near(i, 1 - at.c).wait_send()
    for parcel in (twin_a, twin_b, twin_c, beside_b):
        parcel.sent()
    for out, rows, other_rows, i in (
        (c_out, my_c, span((1 - k) * HALF, HALF), 0),
        (b_out, my_b, span((1 - at.c) * HALF, HALF), 1),
        (a_out, my_quarter, span(at.xh * HALF + (1 - at.c) * QUARTER, QUARTER), 2),
        (a_out, far_quarter, span((1 - at.xh) * HALF + (1 - at.c) * QUARTER, QUARTER), 3),
    ):
        to_core(out, rows, i).wait_send()
        to_core(out, other_rows, i).wait_recv()


def gradients(scale, bias, a_ids, b_ids, c_ids, a, b, c):
    vmem = pl.BlockSpec(memory_space=pltpu.VMEM)
    smem = pl.BlockSpec(memory_space=pltpu.SMEM)
    hbm = pl.BlockSpec(memory_space=pl.ANY)
    out = jax.ShapeDtypeStruct((ROWS, WIDTH), jnp.float32)
    dma = pltpu.SemaphoreType.DMA
    f32, bf16, i16 = jnp.float32, jnp.bfloat16, jnp.int16
    m = pltpu.VMEM
    return pl.pallas_call(
        kernel,
        out_shape=(out, out, out),
        in_specs=[smem, smem] + [vmem] * 4 + [hbm] * 3,
        out_specs=(vmem, vmem, vmem),
        scratch_shapes=[
            m((BLOCK, WIDTH), bf16), m((BLOCK, WIDTH), bf16), m((BLOCK, WIDTH), bf16),
            m((BLOCK, WIDTH), f32), m((BLOCK, WIDTH), f32), m((BLOCK, WIDTH), f32),
            m((BLOCK, BLOCK), bf16), m((BLOCK, BLOCK), bf16), m((BLOCK, BLOCK), bf16),
            m((8, QUARTER, WIDTH), f32),
            m((2, 7, QUARTER, WIDTH), i16), m((2, 7, 8, 128), f32),
            m((2, 2, 3, HALF, WIDTH), i16), m((2, 2, 3, 8, 128), f32),
            m((2, 7, HALF, WIDTH), i16), m((2, 7, 8, 128), f32),
            m((2, 4, HALF, WIDTH), i16), m((2, 4, 8, 128), f32),
            m((HALF, WIDTH), f32),
            dma((2, 4)), dma((2, 4)), dma((2, 2, 2)), dma((2, 2, 2)), dma((2, 4)), dma((2, 4)),
            dma((7,)), dma((7,)), dma((1,)), dma((1,)), dma((3,)),
            dma((7, 2)), dma((7, 2)), dma((2, 3, 2)), dma((2, 3, 2)), dma((7, 2)), dma((7, 2)),
            dma((8,)), dma((8,)), dma((4, 2)), dma((4, 2)), dma((4,)), dma((4,)),
        ],
        compiler_params=pltpu.CompilerParams(
            collective_id=0, has_side_effects=True, vmem_limit_bytes=56 << 20
        ),
    )(
        scale, bias, a_ids.reshape(BLOCK, 1), a_ids.reshape(1, BLOCK),
        b_ids.reshape(1, BLOCK), c_ids.reshape(BLOCK, 1), a, b, c,
    )


def body(event, lidar, frame, sample_ids, logit_scale, logit_bias):
    at = Place()
    blocked = sample_ids.reshape(3, 64, 2, HALF)

    def ids(which, half, shards):
        return jnp.concatenate(
            [lax.dynamic_slice(blocked, (which, d, half, 0), (1, 1, 1, HALF)).reshape(HALF) for d in shards]
        )

    def diagonal(o):
        s = (at.s + o + 8) % 8
        return at.at(xl=s // 4, y=jnp.where(s < 4, s, 7 - s), z=(at.z + o + 8) % 8)[0]

    a_ids = ids(0, at.xh, [diagonal(o) for o in OFFSETS[8]])
    b_ids = ids(1, at.c, [at.at(xl=xl, y=(at.y + o + 4) % 4)[0] for xl in (at.xl, 1 - at.xl) for o in OFFSETS[4]])
    c_ids = ids(2, (at.c + at.xh) % 2, [at.at(z=(at.z + o + 8) % 8)[0] for o in OFFSETS[8]])
    return gradients(logit_scale, logit_bias, a_ids, b_ids, c_ids, event, lidar, frame)


def solution(mesh):
    placed = (P("dp", None), P("dp", None), P("dp", None), P(), P(), P())
    return jax.shard_map(
        body,
        mesh=mesh,
        in_specs=placed,
        out_specs=(P("dp", None), P("dp", None), P("dp", None)),
        check_vma=False,
    )
```

time: 1040 us -> 120 us (0.12)
  waiting for transfers between devices: 940 us -> 0 us
  Pallas kernels: 0 us -> 109 us
  matrix products: 72.1 us -> 0 us
  between operations: 13.8 us -> 1.31 us
    all_gather x3 -> x0, waiting for transfers between devices: 832 us -> none  [the longest x1 284 us: body(): lax.all_gather(shares[1], 'dp', axis=0, tiled=True)]
    pallas_call x0 -> x1, Pallas kernels: none -> 109 us  [gradients(): pl.pallas_call(kernel, out_shape=(out, out, out), in_specs=[smem, smem] +...]
    psum x1 -> x0, waiting for transfers between devices: 108 us -> none  [body(): return lax.psum((g_event, g_lidar, g_frame), 'group')]
    dot_general x6 -> x0, matrix products: 72.1 us -> none  [body(): jnp.dot(coef, pieces[second], preferred_element_type=jnp.float32)]
  transfers between devices with their start and end apart: 4 -> 0, of which waited for: 4 -> 0; matrix products, arithmetic and copies ran while one was open for 5% -> 0% of each run, Pallas kernels for 0% -> 0%
where the time goes in v2:
time: 120 us; the launch traced here: 119 us
  Pallas kernels  109 us (91%)
  local copies, waits for them, and re-layouts  8.8 us (7%)
  between operations  1.31 us (1%)
    pallas_call x1, Pallas kernels, gradients(): pl.pallas_call(kernel, out_shape=(out, out, out), in_specs=[smem, smem] +...  109 us
    unnamed x9, local copies, waits for them, and re-layouts  5.16 us

profile of v2, /device:TPU:1, one launch (start us, length us, event | category | flops | bytes accessed | tf_op | source)
XLA Modules:
  0.0 119.2 jit_solution(10897378484967016008)
XLA Ops:
  1.0 0.0 copy-start.2
  1.3 0.7 copy-done.2
  2.0 0.3 reshape.93
  2.3 0.1 fusion.23
  2.4 0.1 concatenate.9
  2.5 0.1 concatenate.11
  2.6 0.6 reshape.103.a_row
  3.1 0.1 concatenate.10
  3.2 0.6 reshape.112.b_row
  3.8 0.9 reshape.122.a_col
  4.7 0.9 reshape.123.c_col
  5.6 109.1 %shard_map.85 = (f32[192,1024]{1,0:T(8,128)}, f32[192,1024]{1,0:T(8,128)}, f32[192,1024]{1,0:T(8,128)}) custom-call(f32[3]{0:T(128)} %scale.1, f32[3]{0:T(128)} %bias.1, s32[768,1]{1,0:T(8,128)} %reshape.122.a_col, s32[1,768]{1,0:T(1,128)} %reshape.103.a_row, s32[1,768]{1,0:T(1,128)} %reshape.112.b_row, s32[768,1]{1,0:T(8,128)} %reshape.123.c_col, ...), custom_call_target="tpu_custom_call" | custom-call | tf_op jit(solution)/shard_map/pallas_call | solution.py:404
  114.7 0.0 copy-start.1
  114.7 2.2 %copy.14 = f32[192,1024]{1,0:T(8,128)} copy(f32[192,1024]{1,0:T(8,128)} %get-tuple-element.30) | data formatting | bytes 1572864
  116.9 0.0 copy-done.1
  116.9 0.0 copy-start
  116.9 0.9 copy.15
  117.7 0.5 copy-done
  118.3 0.9 copy.16
  (1 shorter events, 0.0 us)
Async XLA Ops:
  1.0 0.9 copy-start.2
  114.7 2.2 %copy-start.1 = (f32[192,1024]{1,0:T(8,128)S(1)}, f32[192,1024]{1,0:T(8,128)}, u32[]{:S(2)}) copy-start(f32[192,1024]{1,0:T(8,128)} %get-tuple-element.31) | copy-start | bytes 2359300
  116.9 1.4 %copy-start = (f32[192,1024]{1,0:T(8,128)S(1)}, f32[192,1024]{1,0:T(8,128)}, u32[]{:S(2)}) copy-start(f32[192,1024]{1,0:T(8,128)} %get-tuple-element.32) | copy-start | bytes 2359300

commit v3 on v2

v3 whole, which is shorter than its diff:
```python
import math

import jax
import jax.numpy as jnp
from jax import lax
from jax.experimental import pallas as pl
from jax.experimental.pallas import tpu as pltpu
from jax.sharding import PartitionSpec as P

MESH = pl.DeviceIdType.MESH
ROWS = 192
HALF = 96
QUARTER = 48
WIDTH = 1024
BLOCK = 768
TOKENS = 12288
TILE = 256
LOG2E = math.log2(math.e)
OFFSETS = {8: (4, 3, -3, 2, -2, 1, -1, 0), 4: (2, 1, -1, 0)}

ORDER = (
    "sP", "sA", "sC", "sX", "X", "C1", "A1", "A2", "Q1", "C2", "P1", "C3", "A3", "cb2", "ab3", "cb3",
    "A4", "C4", "ab2", "ab1", "ab0", "cb1", "ca1", "c0n1", "cb0", "c1n1", "ca0", "c1f1", "bc0", "ca3",
    "c0f1", "bc1", "b0f1", "b0n1", "ca2", "ac0", "c1f2", "ns0", "c1n2", "an1", "c0f2", "ac1", "af1",
    "b1f1", "ns1", "c0n2", "ac2", "bc2", "b0f2", "c1f3", "c0f3", "ns2", "b1n1", "af2", "c1f4", "b1f2",
    "c1n3", "Lb0", "xf1", "c0n3", "an2", "c0f4", "Lc1", "af3", "Lb1", "xn1", "xf2", "af4", "an3", "Lc0",
    "Sc1", "Lx", "La", "Ob", "Sc0", "Oa",
)


class Place:
    def __init__(self):
        dp, group = lax.axis_index("dp"), lax.axis_index("group")
        self.xl, self.y, self.z = dp // 32, (dp // 8) % 4, dp % 8
        self.xh, self.c = group // 2, group % 2
        self.s = jnp.where(self.xl == 0, self.y, 7 - self.y)

    def at(self, xh=None, xl=None, y=None, z=None, c=None):
        xh, xl = self.xh if xh is None else xh, self.xl if xl is None else xl
        y, z = self.y if y is None else y, self.z if z is None else z
        c = self.c if c is None else c
        return (xl * 32 + y * 8 + z, xh * 2 + c)

    def column(self, step):
        return self.at(z=(self.z + step + 8) % 8)

    def row(self, step):
        return self.at(y=(self.y + step + 4) % 4)

    def diagonal(self, step):
        s = (self.s + step + 8) % 8
        return self.at(
            xl=s // 4, y=jnp.where(s < 4, s, 7 - s), z=(self.z + step + 8) % 8
        )

    def line(self, step):
        x = (self.xh * 2 + self.xl + step + 4) % 4
        return self.at(xh=x // 2, xl=x % 2)

    def beside(self):
        return self.at(xl=1 - self.xl)

    def other_core(self):
        return self.at(c=1 - self.c)

    def twin(self, other=False):
        return self.at(xh=1 - self.xh, c=1 - self.c if other else self.c)


def remote(src, dst, send, recv, device):
    return pltpu.make_async_remote_copy(
        src_ref=src,
        dst_ref=dst,
        send_sem=send,
        recv_sem=recv,
        device_id=device,
        device_id_type=MESH,
    )


def slot(n, offset):
    return OFFSETS[n].index(n // 2 if offset == -(n // 2) else offset)


class RingGather:
    def __init__(self, n, neighbour, far, own, view, send, recv):
        self.n, self.neighbour, self.far, self.own = n, neighbour, far, own
        self.view, self.send, self.recv = view, send, recv

    def reach(self, direction):
        return self.n // 2 if direction == self.far else self.n // 2 - 1

    def copy(self, direction, step):
        d = 0 if direction == self.far else 1
        src = self.own if step == 1 else self.view(slot(self.n, -direction * (step - 1)))
        return remote(
            src,
            self.view(slot(self.n, -direction * step)),
            self.send.at[d, step - 1],
            self.recv.at[d, step - 1],
            self.neighbour(direction),
        )

    def start(self):
        for direction in (self.far, -self.far):
            self.copy(direction, 1).start()

    def stage(self, step, arrived=None):
        for direction in (self.far, -self.far):
            if step <= self.reach(direction):
                self.copy(direction, step).wait_recv()
                if step < self.reach(direction):
                    self.copy(direction, step + 1).start()
                if arrived is not None:
                    arrived(slot(self.n, -direction * step))

    def finish(self):
        for direction in (self.far, -self.far):
            for step in range(1, self.reach(direction) + 1):
                self.copy(direction, step).wait_send()


class Parcel:
    def __init__(self, out, out_scale, into, into_scale, send, recv, device):
        self.out, self.out_scale = out, out_scale
        self.into, self.into_scale = into, into_scale
        self.data = remote(out, into, send.at[0], recv.at[0], device)
        self.scale = remote(out_scale, into_scale, send.at[1], recv.at[1], device)

    def pack(self, value):
        top = jnp.max(jnp.abs(value), axis=0, keepdims=True)
        top = jnp.maximum(jnp.max(top, axis=1, keepdims=True), 1e-30)
        self.out[...] = (
            jnp.round(value * (32767.0 / top)).astype(jnp.int32).astype(jnp.int16)
        )
        self.out_scale[...] = jnp.broadcast_to(top * (1 / 32767.0), (8, 128))

    def go(self):
        self.data.start()
        self.scale.start()

    def start(self, value):
        self.pack(value)
        self.go()

    def arrive(self):
        self.data.wait_recv()
        self.scale.wait_recv()

    def take(self):
        self.arrive()
        return self.into[...].astype(jnp.int32).astype(jnp.float32) * self.into_scale[0:1, 0:1]

    def sent(self):
        self.data.wait_send()
        self.scale.wait_send()


class RingReduce:
    def __init__(self, n, neighbour, far, part, box):
        self.n, self.neighbour, self.far, self.part, self.box = n, neighbour, far, part, box

    def steps(self, direction):
        return self.n // 2 if direction == self.far else self.n // 2 - 1

    def parcel(self, direction, step):
        out, out_scale, into, into_scale, send, recv = self.box
        i = step - 1 if direction == self.far else self.n // 2 + step - 1
        return Parcel(
            out.at[i], out_scale.at[i], into.at[i], into_scale.at[i],
            send.at[i], recv.at[i], self.neighbour(direction),
        )

    def step(self, direction, step):
        if step > self.steps(direction):
            return
        value = self.part(slot(self.n, direction * (self.steps(direction) + 1 - step)))
        if step > 1:
            value = value + self.parcel(direction, step - 1).take()
        self.parcel(direction, step).start(value)

    def both(self, step):
        self.step(self.far, step)
        self.step(-self.far, step)

    def last(self):
        value = self.part(slot(self.n, 0))
        for direction in (self.far, -self.far):
            value = value + self.parcel(direction, self.steps(direction)).take()
        return value

    def finish(self):
        for direction in (self.far, -self.far):
            for step in range(1, self.steps(direction) + 1):
                self.parcel(direction, step).sent()


def greet(at, meanwhile):
    barrier = pltpu.get_barrier_semaphore()
    others = [at.column(-1), at.column(1), at.diagonal(-1), at.diagonal(1), at.row(-1), at.row(1)]
    others += [at.line(-1), at.line(1), at.other_core(), at.twin(), at.twin(True)]
    for device in others:
        pl.semaphore_signal(barrier, inc=1, device_id=device, device_id_type=MESH)
    meanwhile()
    pl.semaphore_wait(barrier, len(others))


def coefficients(rows, cols, row_ids, col_ids, scale, bias):
    logits = lax.dot_general(
        rows, cols, (((1,), (1,)), ((), ())), preferred_element_type=jnp.float32
    )
    power = jnp.minimum(logits * (scale * -LOG2E) - bias * LOG2E, 126.0)
    sigmoid = 1.0 / (1.0 + jnp.exp2(power))
    label = jnp.where(row_ids == col_ids, 1.0, 0.0)
    return (sigmoid - label).astype(jnp.bfloat16)


def product(coef, rows):
    return jnp.dot(coef, rows, preferred_element_type=jnp.float32)


def product_t(coef, rows):
    return lax.dot_general(
        coef, rows, (((0,), (0,)), ((), ())), preferred_element_type=jnp.float32
    )


def kernel(
    scale, bias, all_ids, a_own, b_own, c_own, a_out, b_out, c_out, a_unit, b_unit, c_unit, ids, ids_t,
    a, b, c, ga, gb, gc, coef_ab, coef_ca, coef_cb,
    a_near, a_box, a_box_scale, b_box, b_box_scale, c_box, c_box_scale, x_box, x_box_scale, sums,
    ga_send, ga_recv, gb_send, gb_recv, gc_send, gc_recv, gt_send, gt_recv, gx_send, gx_recv, gw_send, gw_recv, own_sem,
    ra_send, ra_recv, rb_send, rb_recv, rc_send, rc_recv, rx_send, rx_recv, rt_send, rt_recv, re_send, re_recv,
):
    at = Place()

    def span(start, size):
        return pl.ds(pl.multiple_of(start, 16), size)

    k = (at.c + at.xh) % 2
    my_b, my_c, my_a = span(at.c * HALF, HALF), span(k * HALF, HALF), span(at.xh * HALF, HALF)
    my_quarter = span(at.xh * HALF + at.c * QUARTER, QUARTER)

    def a_quarter(i, core):
        return a.at[span(i * HALF + core * QUARTER, QUARTER)]

    def piece(ref, i):
        return ref.at[i * HALF : (i + 1) * HALF]

    def c_quarter(i, part):
        return c.at[span(i * HALF + part * QUARTER, QUARTER)]

    my_part = span(k * HALF + at.xh * QUARTER, QUARTER)
    ring_c = RingGather(8, at.column, 1, c_own.at[my_part], lambda i: c_quarter(i, at.xh), gc_send, gc_recv)
    ring_a = RingGather(8, at.diagonal, -1, a_own.at[my_quarter], lambda i: a_quarter(i, at.c), ga_send, ga_recv)
    ring_b = [
        RingGather(4, at.row, 1, b_own.at[my_b], lambda i: piece(b, i), gb_send.at[0], gb_recv.at[0]),
        RingGather(4, at.row, -1, piece(b, 7), lambda i: piece(b, 4 + i), gb_send.at[1], gb_recv.at[1]),
    ]
    beside = remote(b_own.at[my_b], piece(b, 7), gx_send.at[0], gx_recv.at[0], at.beside())
    own = [
        pltpu.make_async_copy(a_own.at[my_a], piece(a, 7), own_sem.at[0]),
        pltpu.make_async_copy(b_own.at[my_b], piece(b, 3), own_sem.at[1]),
        pltpu.make_async_copy(c_own.at[my_c], piece(c, 7), own_sem.at[2]),
    ]

    def pass_over(i, core):
        view = a_quarter(i, core)
        return remote(view, view, gt_send.at[i], gt_recv.at[i], at.other_core())

    def share(i, part):
        view = c_quarter(i, part)
        return remote(view, view, gw_send.at[i], gw_recv.at[i], at.twin(True))

    done = set()

    def once(key, wait):
        if key not in done:
            done.add(key)
            wait()

    def to_other(i):
        pass_over(i, at.c).start()

    def gather_a(step):
        ring_a.stage(step, to_other)

    def gather_c(step):
        ring_c.stage(step, lambda i: share(i, at.xh).start())

    def x_done():
        beside.wait_recv()
        ring_b[1].start()

    def a_here(*groups):
        once("own", lambda: [copy.wait() for copy in own])
        for i in (i for g in groups or range(4) for i in (2 * g, 2 * g + 1)):
            if i < 7:
                once(("a", i), lambda: pass_over(i, 1 - at.c).wait_recv())

    def b_here():
        once("own", lambda: [copy.wait() for copy in own])
        for r in range(2):
            once(("b", r), lambda: ring_b[r].stage(2))

    def c_here(g):
        once("own", lambda: [copy.wait() for copy in own])
        for i in (2 * g, 2 * g + 1):
            if i < 7:
                once(("c", i), lambda: share(i, 1 - at.xh).wait_recv())

    def ab_rows(g):
        a_here(g)
        b_here()
        rows = pl.ds(g * ROWS, ROWS)
        tile = coefficients(a[rows, :], b[...], ids_t[rows, 0:1], ids[1:2, 0:BLOCK], scale[0], bias[0])
        coef_ab[rows, :] = tile
        ga[rows, :] = scale[0] * product(tile, b[...])

    def cb_rows(g):
        b_here()
        c_here(g)
        rows = pl.ds(g * ROWS, ROWS)
        tile = coefficients(c[rows, :], b[...], ids_t[rows, 2:3], ids[1:2, 0:BLOCK], scale[2], bias[2])
        coef_cb[rows, :] = tile
        gc[rows, :] = scale[2] * product(tile, b[...])

    def ca_rows(g):
        a_here()
        c_here(g)
        rows = pl.ds(g * ROWS, ROWS)
        tile = coefficients(c[rows, :], a[...], ids_t[rows, 2:3], ids[0:1, 0:BLOCK], scale[1], bias[1])
        coef_ca[rows, :] = tile
        gc[rows, :] = gc[rows, :] + scale[1] * product(tile, a[...])

    def a_cols(i):
        cols = pl.ds(i * TILE, TILE)
        ga[cols, :] = ga[cols, :] + scale[1] * product_t(coef_ca[:, cols], c[...])

    def b_cols(i):
        cols = pl.ds(i * TILE, TILE)
        gb[cols, :] = scale[0] * product_t(coef_ab[:, cols], a[...]) + scale[2] * product_t(coef_cb[:, cols], c[...])

    def a_part(i):
        once(("near", i), lambda: near(i, 1 - at.c).wait_recv())
        return ga[pl.ds(pl.multiple_of(i * HALF + at.c * QUARTER, 8), QUARTER), :] + a_near[i]

    reduce_a = RingReduce(
        8, at.diagonal, -1, a_part,
        (a_box.at[0], a_box_scale.at[0], a_box.at[1], a_box_scale.at[1], ra_send, ra_recv),
    )

    def c_ring(q):
        def part(i):
            return gc[i * HALF + q * QUARTER : i * HALF + (q + 1) * QUARTER, :]

        return RingReduce(
            8, at.column, 1, part,
            (c_box.at[0, q], c_box_scale.at[0, q], c_box.at[1, q], c_box_scale.at[1, q], rc_send.at[q], rc_recv.at[q]),
        )

    reduce_c = [c_ring(q) for q in range(2)]
    reduce_b = [
        RingReduce(
            4, at.row, 1 - 2 * r, lambda i, r=r: gb[(4 * r + i) * HALF : (4 * r + i + 1) * HALF, :],
            (b_box.at[0, r], b_box_scale.at[0, r], b_box.at[1, r], b_box_scale.at[1, r], rb_send.at[r], rb_recv.at[r]),
        )
        for r in range(2)
    ]

    def x_part(i):
        next_part = (at.xh + at.xl) % 2
        r, part = ((0, 1 - at.xh), (1, next_part), (1, 1 - next_part), (0, at.xh))[i]
        return sums[r, pl.ds(pl.multiple_of(part * QUARTER, 8), QUARTER), :]

    reduce_x = RingReduce(
        4, at.line, 1, x_part,
        (x_box.at[0], x_box_scale.at[0], x_box.at[1], x_box_scale.at[1], rx_send, rx_recv),
    )

    def near(i, core):
        return remote(
            ga.at[pl.ds(pl.multiple_of(i * HALF + core * QUARTER, 8), QUARTER)], a_near.at[i],
            rt_send.at[i], rt_recv.at[i], at.other_core(),
        )

    def rows_of(half, part):
        return span(half * HALF + part * QUARTER, QUARTER)

    def ready(out, unit, half, part, i, device):
        rows, number = out.at[rows_of(half, part)], unit.at[2 * half + part]
        return Parcel(rows, number, rows, number, re_send.at[i], re_recv.at[i], device)

    def to_twin(i):
        if i < 2:
            return ready(c_out.at[at.xh], c_unit.at[at.xh], k, i, i, at.twin(True))
        if i == 2:
            return ready(b_out, b_unit, at.c, at.xh, i, at.twin())
        return ready(a_out, a_unit, at.xh, at.c, i, at.twin())

    def from_twin(i):
        if i < 2:
            return ready(c_out.at[1 - at.xh], c_unit.at[1 - at.xh], k, i, i, at.twin(True))
        if i == 2:
            return ready(b_out, b_unit, at.c, 1 - at.xh, i, at.twin())
        return ready(a_out, a_unit, 1 - at.xh, at.c, i, at.twin())

    def to_core(i, other):
        chip = 1 - at.xh if other else at.xh
        j = 4 + 2 * i + other
        if i < 2:
            return ready(c_out.at[chip], c_unit.at[chip], k, i, j, at.other_core())
        if i == 2:
            return ready(b_out, b_unit, at.c, chip, j, at.other_core())
        return ready(a_out, a_unit, chip, at.c, j, at.other_core())

    def from_core(i, other):
        chip = 1 - at.xh if other else at.xh
        j = 4 + 2 * i + other
        if i < 2:
            return ready(c_out.at[chip], c_unit.at[chip], 1 - k, i, j, at.other_core())
        if i == 2:
            return ready(b_out, b_unit, 1 - at.c, chip, j, at.other_core())
        return ready(a_out, a_unit, chip, 1 - at.c, j, at.other_core())

    def mine_done(i, value):
        to_twin(i).start(value)
        to_core(i, 0).go()

    def other_done(i):
        from_twin(i).arrive()
        to_core(i, 1).go()

    def near_go(i):
        for j in ((0, 1), (2, 3, 4), (5, 6, 7))[i]:
            near(j, 1 - at.c).start()

    def b_last(r):
        sums[r] = reduce_b[r].last()

    steps = {
        "sA": ring_a.start,
        "sC": ring_c.start,
        "sX": beside.start,
        "sP": ring_b[0].start,
        "X": x_done,
        "P1": lambda: ring_b[0].stage(1),
        "Q1": lambda: ring_b[1].stage(1),
        "La": lambda: mine_done(3, reduce_a.last()),
        "Lx": lambda: mine_done(2, reduce_x.last()),
        "Oa": lambda: other_done(3),
        "Ob": lambda: other_done(2),
    }
    for i in range(1, 5):
        steps[f"A{i}"] = lambda i=i: gather_a(i)
        steps[f"C{i}"] = lambda i=i: gather_c(i)
    for i in range(4):
        steps[f"ab{i}"] = lambda i=i: ab_rows(i)
        steps[f"cb{i}"] = lambda i=i: cb_rows(i)
        steps[f"ca{i}"] = lambda i=i: ca_rows(i)
    for i in range(3):
        steps[f"ac{i}"] = lambda i=i: a_cols(i)
        steps[f"bc{i}"] = lambda i=i: b_cols(i)
        steps[f"ns{i}"] = lambda i=i: near_go(i)
    for q in range(2):
        steps[f"Lb{q}"] = lambda q=q: b_last(q)
        steps[f"Lc{q}"] = lambda q=q: mine_done(q, reduce_c[q].last())
        steps[f"Sc{q}"] = lambda q=q: other_done(q)
    for name, ring in (("a", reduce_a), ("b0", reduce_b[0]), ("b1", reduce_b[1]), ("c0", reduce_c[0]), ("c1", reduce_c[1]), ("x", reduce_x)):
        for way, direction in (("f", ring.far), ("n", -ring.far)):
            for i in range(1, ring.steps(direction) + 1):
                steps[f"{name}{way}{i}"] = lambda ring=ring, d=direction, i=i: ring.step(d, i)

    def shards_of(which):
        if which == 0:
            return [at.diagonal(o)[0] for o in OFFSETS[8]], at.xh
        if which == 1:
            return [at.at(xl=xl, y=(at.y + o + 4) % 4)[0] for xl in (at.xl, 1 - at.xl) for o in OFFSETS[4]], at.c
        return [at.column(o)[0] for o in OFFSETS[8]], k

    def lay_out_ids():
        ids[...] = jnp.zeros_like(ids)
        lane = lax.broadcasted_iota(jnp.int32, (3, 256), 1)
        row = lax.broadcasted_iota(jnp.int32, (3, 256), 0)
        for which in range(3):
            shards, half = shards_of(which)
            for i, shard in enumerate(shards):
                base = shard * ROWS + half * HALF
                start = base // 128 * 128 - base // (TOKENS - HALF) * 128
                window = all_ids[:, pl.ds(pl.multiple_of(start, 128), 256)]
                first = i * HALF % 128
                moved = pltpu.roll(window, (first - base + start + 256) % 256, 1)
                here = (row == which) & (lane >= first) & (lane < first + HALF)
                place = (slice(0, 3), slice(i * HALF - first, i * HALF - first + 256))
                ids[place] = jnp.where(here, moved, ids[place])
        ids_t[...] = jnp.transpose(ids[:, 0:BLOCK])

    for copy in own:
        copy.start()
    greet(at, lay_out_ids)
    for name in ORDER:
        steps[name]()

    for ring in (ring_a, ring_c, *ring_b, reduce_a, reduce_x, *reduce_c, *reduce_b):
        ring.finish()
    beside.wait_send()
    for i in range(7):
        pass_over(i, at.c).wait_send()
        share(i, at.xh).wait_send()
    for i in range(8):
        near(i, 1 - at.c).wait_send()
    for i in range(4):
        to_twin(i).sent()
        for other in range(2):
            to_core(i, other).sent()
            from_core(i, other).arrive()


def gradients(scale, bias, ids, a, b, c):
    vmem = pl.BlockSpec(memory_space=pltpu.VMEM)
    smem = pl.BlockSpec(memory_space=pltpu.SMEM)
    hbm = pl.BlockSpec(memory_space=pl.ANY)
    dma = pltpu.SemaphoreType.DMA
    f32, bf16, i16 = jnp.float32, jnp.bfloat16, jnp.int16
    m = pltpu.VMEM
    shape = jax.ShapeDtypeStruct
    a, b, c, a_unit, b_unit, c_unit = pl.pallas_call(
        kernel,
        out_shape=(
            shape((ROWS, WIDTH), i16), shape((ROWS, WIDTH), i16), shape((2, ROWS, WIDTH), i16),
            shape((4, 8, 128), f32), shape((4, 8, 128), f32), shape((2, 4, 8, 128), f32),
        ),
        in_specs=[smem, smem, vmem] + [hbm] * 3,
        out_specs=(vmem,) * 6,
        scratch_shapes=[
            m((8, 896), jnp.int32), m((BLOCK, 8), jnp.int32),
            m((BLOCK, WIDTH), bf16), m((BLOCK, WIDTH), bf16), m((BLOCK, WIDTH), bf16),
            m((BLOCK, WIDTH), f32), m((BLOCK, WIDTH), f32), m((BLOCK, WIDTH), f32),
            m((BLOCK, BLOCK), bf16), m((BLOCK, BLOCK), bf16), m((BLOCK, BLOCK), bf16),
            m((8, QUARTER, WIDTH), f32),
            m((2, 7, QUARTER, WIDTH), i16), m((2, 7, 8, 128), f32),
            m((2, 2, 3, HALF, WIDTH), i16), m((2, 2, 3, 8, 128), f32),
            m((2, 2, 7, QUARTER, WIDTH), i16), m((2, 2, 7, 8, 128), f32),
            m((2, 3, QUARTER, WIDTH), i16), m((2, 3, 8, 128), f32),
            m((2, HALF, WIDTH), f32),
            dma((2, 4)), dma((2, 4)), dma((2, 2, 2)), dma((2, 2, 2)), dma((2, 4)), dma((2, 4)),
            dma((7,)), dma((7,)), dma((1,)), dma((1,)), dma((7,)), dma((7,)), dma((3,)),
            dma((7, 2)), dma((7, 2)), dma((2, 3, 2)), dma((2, 3, 2)), dma((2, 7, 2)), dma((2, 7, 2)), dma((3, 2)), dma((3, 2)),
            dma((8,)), dma((8,)), dma((12, 2)), dma((12, 2)),
        ],
        compiler_params=pltpu.CompilerParams(
            collective_id=0, has_side_effects=True, vmem_limit_bytes=56 << 20
        ),
    )(scale, bias, ids, a, b, c)
    return decode(a, b, c, a_unit, b_unit, c_unit)


def decode_kernel(a, b, c, a_unit, b_unit, c_unit, a_out, b_out, c_out):
    def value(code, unit):
        return code.astype(jnp.int32).astype(jnp.float32) * unit[0:1, 0:1]

    for i in range(4):
        rows = pl.ds(i * QUARTER, QUARTER)
        a_out[rows, :] = value(a[rows, :], a_unit[i])
        b_out[rows, :] = value(b[rows, :], b_unit[i])
        c_out[rows, :] = value(c[0, rows, :], c_unit[0, i]) + value(c[1, rows, :], c_unit[1, i])


def decode(a, b, c, a_unit, b_unit, c_unit):
    vmem = pl.BlockSpec(memory_space=pltpu.VMEM)
    out = jax.ShapeDtypeStruct((ROWS, WIDTH), jnp.float32)
    return pl.pallas_call(
        decode_kernel,
        out_shape=(out, out, out),
        in_specs=[vmem] * 6,
        out_specs=(vmem, vmem, vmem),
    )(a, b, c, a_unit, b_unit, c_unit)


def body(event, lidar, frame, sample_ids, logit_scale, logit_bias):
    return gradients(logit_scale, logit_bias, sample_ids, event, lidar, frame)


def solution(mesh):
    placed = (P("dp", None), P("dp", None), P("dp", None), P(), P(), P())
    return jax.shard_map(
        body,
        mesh=mesh,
        in_specs=placed,
        out_specs=(P("dp", None), P("dp", None), P("dp", None)),
        check_vma=False,
    )
```

time: 120 us -> 98.1 us (0.82)
  the two profiles are of different devices: /device:TPU:1 before, /device:TPU:9 now
where the time goes in v3:
time: 98.1 us; the launch traced here: 98 us
  Pallas kernels  97.3 us (99%)
    pallas_call x1, Pallas kernels, gradients(): pl.pallas_call(kernel, out_shape=(shape((ROWS, WIDTH), i16), shape((ROWS,...  94.1 us
    pallas_call x1, Pallas kernels, decode(): pl.pallas_call(decode_kernel, out_shape=(out, out, out), in_specs=[vmem]...  3.25 us

profile of v3, /device:TPU:9, one launch (start us, length us, event | category | flops | bytes accessed | tf_op | source)
XLA Modules:
  0.0 98.0 jit_solution(15119422930392114398)
XLA Ops:
  0.6 94.1 %shard_map.85 = (s16[192,1024]{1,0:T(8,128)(2,1)}, s16[192,1024]{1,0:T(8,128)(2,1)}, s16[2,192,1024]{2,1,0:T(8,128)(2,1)}, f32[4,8,128]{2,1,0:T(8,128)}, f32[4,8,128]{2,1,0:T(8,128)}, /*index=5*/f32[2,4,8,128]{3,2,1,0:T(8,128)}) custom-call(f32[3]{0:T(128)} %scale.1, f32[3]{0:T(128)} %bias.1, s32[3,12288]{1,0:T(4,128)} %all_ids.1, bf16[192,1024]{1,0:T(8,128)(2,1)} %a_own.1, ...), custom_call_target="tpu_custom_call" | custom-call | tf_op jit(solution)/shard_map/pallas_call | solution.py:527
  94.7 3.3 %shard_map.86 = (f32[192,1024]{1,0:T(8,128)}, f32[192,1024]{1,0:T(8,128)}, f32[192,1024]{1,0:T(8,128)}) custom-call(s16[192,1024]{1,0:T(8,128)(2,1)} %get-tuple-element.9.a, s16[192,1024]{1,0:T(8,128)(2,1)} %get-tuple-element.10.b, s16[2,192,1024]{2,1,0:T(8,128)(2,1)} %get-tuple-element.11.c, f32[4,8,128]{2,1,0:T(8,128)} %get-tuple-element.12.a_unit, ...), custom_call_target="tpu_custom_call" | custom-call | tf_op jit(solution)/shard_map/pallas_call | solution.py:572

commit v4 on v3

--- a/solution.py
+++ b/solution.py
@@ -19,12 +19,12 @@
 OFFSETS = {8: (4, 3, -3, 2, -2, 1, -1, 0), 4: (2, 1, -1, 0)}
 
 ORDER = (
-    "sP", "sA", "sC", "sX", "X", "C1", "A1", "A2", "Q1", "C2", "P1", "C3", "A3", "cb2", "ab3", "cb3",
-    "A4", "C4", "ab2", "ab1", "ab0", "cb1", "ca1", "c0n1", "cb0", "c1n1", "ca0", "c1f1", "bc0", "ca3",
-    "c0f1", "bc1", "b0f1", "b0n1", "ca2", "ac0", "c1f2", "ns0", "c1n2", "an1", "c0f2", "ac1", "af1",
-    "b1f1", "ns1", "c0n2", "ac2", "bc2", "b0f2", "c1f3", "c0f3", "ns2", "b1n1", "af2", "c1f4", "b1f2",
-    "c1n3", "Lb0", "xf1", "c0n3", "an2", "c0f4", "Lc1", "af3", "Lb1", "xn1", "xf2", "af4", "an3", "Lc0",
-    "Sc1", "Lx", "La", "Ob", "Sc0", "Oa",
+    "sC", "sP", "sX", "sA", "sD", "P1", "D1", "C1", "P2", "A1", "C2", "A2", "ab2", "D2", "cb3", "A3",
+    "C3", "ab3", "cb2", "ab1", "D3", "A4", "cb1", "C4", "ab0", "ca1", "D4", "cb0", "ca0", "c1f1", "bc1",
+    "bc0", "x0f1", "c0f1", "c0n1", "bc2", "x0n1", "ca2", "c1f2", "ca3", "ac0", "c1n1", "x1f1", "ns0",
+    "c0f2", "af1", "x0f2", "c1f3", "c0n2", "ac1", "c1n2", "ac2", "an1", "ns1", "c1f4", "af2", "Lx0",
+    "yf1", "x1n1", "ns2", "c0f3", "x1f2", "c1n3", "an2", "af3", "c0n3", "c0f4", "yf2", "Lx1", "Lc1",
+    "an3", "yn1", "af4", "Lc0", "Ly", "Sc1", "La", "Sc0", "Ob", "Oa",
 )
 
 
@@ -56,9 +56,6 @@
     def line(self, step):
         x = (self.xh * 2 + self.xl + step + 4) % 4
         return self.at(xh=x // 2, xl=x % 2)
-
-    def beside(self):
-        return self.at(xl=1 - self.xl)
 
     def other_core(self):
         return self.at(c=1 - self.c)
@@ -228,9 +225,9 @@
 def kernel(
     scale, bias, all_ids, a_own, b_own, c_own, a_out, b_out, c_out, a_unit, b_unit, c_unit, ids, ids_t,
     a, b, c, ga, gb, gc, coef_ab, coef_ca, coef_cb,
-    a_near, a_box, a_box_scale, b_box, b_box_scale, c_box, c_box_scale, x_box, x_box_scale, sums,
-    ga_send, ga_recv, gb_send, gb_recv, gc_send, gc_recv, gt_send, gt_recv, gx_send, gx_recv, gw_send, gw_recv, own_sem,
-    ra_send, ra_recv, rb_send, rb_recv, rc_send, rc_recv, rx_send, rx_recv, rt_send, rt_recv, re_send, re_recv,
+    a_near, a_box, a_box_scale, b_box, b_box_scale, c_box, c_box_scale, y_box, y_box_scale, sums,
+    ga_send, ga_recv, gb_send, gb_recv, gc_send, gc_recv, gt_send, gt_recv, gx_send, gx_recv, own_sem,
+    ra_send, ra_recv, rb_send, rb_recv, rc_send, rc_recv, ry_send, ry_recv, rt_send, rt_recv, re_send, re_recv,
 ):
     at = Place()
 
@@ -247,17 +244,22 @@
     def piece(ref, i):
         return ref.at[i * HALF : (i + 1) * HALF]
 
-    def c_quarter(i, part):
-        return c.at[span(i * HALF + part * QUARTER, QUARTER)]
-
-    my_part = span(k * HALF + at.xh * QUARTER, QUARTER)
-    ring_c = RingGather(8, at.column, 1, c_own.at[my_part], lambda i: c_quarter(i, at.xh), gc_send, gc_recv)
+    def quarter(ref, i, part):
+        return ref.at[span(i * HALF + part * QUARTER, QUARTER)]
+
+    def c_gather(q):
+        own = c_own.at[span(k * HALF + q * QUARTER, QUARTER)]
+        return RingGather(8, at.column, 1, own, lambda i: quarter(c, i, q), gc_send.at[q], gc_recv.at[q])
+
+    def b_gather(q):
+        return RingGather(4, at.row, 1 - 2 * q, b_share(q), lambda i: quarter(b, i, q), gb_send.at[q], gb_recv.at[q])
+
+    def b_share(q):
+        return b_own.at[span(at.c * HALF + q * QUARTER, QUARTER)]
+
+    ring_c = [c_gather(q) for q in range(2)]
+    ring_b = [b_gather(q) for q in range(2)]
     ring_a = RingGather(8, at.diagonal, -1, a_own.at[my_quarter], lambda i: a_quarter(i, at.c), ga_send, ga_recv)
-    ring_b = [
-        RingGather(4, at.row, 1, b_own.at[my_b], lambda i: piece(b, i), gb_send.at[0], gb_recv.at[0]),
-        RingGather(4, at.row, -1, piece(b, 7), lambda i: piece(b, 4 + i), gb_send.at[1], gb_recv.at[1]),
-    ]
-    beside = remote(b_own.at[my_b], piece(b, 7), gx_send.at[0], gx_recv.at[0], at.beside())
     own = [
         pltpu.make_async_copy(a_own.at[my_a], piece(a, 7), own_sem.at[0]),
         pltpu.make_async_copy(b_own.at[my_b], piece(b, 3), own_sem.at[1]),
@@ -268,9 +270,9 @@
         view = a_quarter(i, core)
         return remote(view, view, gt_send.at[i], gt_recv.at[i], at.other_core())
 
-    def share(i, part):
-        view = c_quarter(i, part)
-        return remote(view, view, gw_send.at[i], gw_recv.at[i], at.twin(True))
+    def over_x(i, q):
+        src = b_share(q) if i == 3 else quarter(b, i, q)
+        return remote(src, quarter(b, 4 + i, q), gx_send.at[q, i], gx_recv.at[q, i], at.line(1 - 2 * q))
 
     done = set()
 
@@ -285,12 +287,17 @@
     def gather_a(step):
         ring_a.stage(step, to_other)
 
-    def gather_c(step):
-        ring_c.stage(step, lambda i: share(i, at.xh).start())
-
-    def x_done():
-        beside.wait_recv()
-        ring_b[1].start()
+    def gather_b(step):
+        for q in range(2):
+            ring_b[q].stage(step, lambda i: over_x(i, q).start())
+
+    def b_start():
+        for q in range(2):
+            ring_b[q].start()
+
+    def x_start():
+        for q in range(2):
+            over_x(3, q).start()
 
     def a_here(*groups):
         once("own", lambda: [copy.wait() for copy in own])
@@ -300,14 +307,12 @@
 
     def b_here():
         once("own", lambda: [copy.wait() for copy in own])
-        for r in range(2):
-            once(("b", r), lambda: ring_b[r].stage(2))
+        for i in range(4):
+            for q in range(2):
+                once(("b", i, q), lambda: over_x(i, q).wait_recv())
 
     def c_here(g):
         once("own", lambda: [copy.wait() for copy in own])
-        for i in (2 * g, 2 * g + 1):
-            if i < 7:
-                once(("c", i), lambda: share(i, 1 - at.xh).wait_recv())
 
     def ab_rows(g):
         a_here(g)
@@ -360,22 +365,25 @@
         )
 
     reduce_c = [c_ring(q) for q in range(2)]
-    reduce_b = [
-        RingReduce(
-            4, at.row, 1 - 2 * r, lambda i, r=r: gb[(4 * r + i) * HALF : (4 * r + i + 1) * HALF, :],
-            (b_box.at[0, r], b_box_scale.at[0, r], b_box.at[1, r], b_box_scale.at[1, r], rb_send.at[r], rb_recv.at[r]),
+    def x_ring(h):
+        next_part = (at.xh + at.xl) % 2
+        places = ((0, 1 - at.xh), (1, next_part), (1, 1 - next_part), (0, at.xh))
+
+        def part(i):
+            r, quarter_of = places[i]
+            return jnp.concatenate(
+                [gb[pl.ds(pl.multiple_of((4 * r + 2 * h + j) * HALF + quarter_of * QUARTER, 8), QUARTER), :] for j in range(2)]
+            )
+
+        return RingReduce(
+            4, at.line, 1 - 2 * h, part,
+            (b_box.at[0, h], b_box_scale.at[0, h], b_box.at[1, h], b_box_scale.at[1, h], rb_send.at[h], rb_recv.at[h]),
         )
-        for r in range(2)
-    ]
-
-    def x_part(i):
-        next_part = (at.xh + at.xl) % 2
-        r, part = ((0, 1 - at.xh), (1, next_part), (1, 1 - next_part), (0, at.xh))[i]
-        return sums[r, pl.ds(pl.multiple_of(part * QUARTER, 8), QUARTER), :]
-
-    reduce_x = RingReduce(
-        4, at.line, 1, x_part,
-        (x_box.at[0], x_box_scale.at[0], x_box.at[1], x_box_scale.at[1], rx_send, rx_recv),
+
+    reduce_x = [x_ring(h) for h in range(2)]
+    reduce_y = RingReduce(
+        4, at.row, 1, lambda i: sums[i // 2, i % 2 * QUARTER : (i % 2 + 1) * QUARTER, :],
+        (y_box.at[0], y_box_scale.at[0], y_box.at[1], y_box_scale.at[1], ry_send, ry_recv),
     )
 
     def near(i, core):
@@ -436,24 +444,25 @@
             near(j, 1 - at.c).start()
 
     def b_last(r):
-        sums[r] = reduce_b[r].last()
+        sums[r] = reduce_x[r].last()
 
     steps = {
         "sA": ring_a.start,
-        "sC": ring_c.start,
-        "sX": beside.start,
-        "sP": ring_b[0].start,
-        "X": x_done,
-        "P1": lambda: ring_b[0].stage(1),
-        "Q1": lambda: ring_b[1].stage(1),
+        "sC": ring_c[0].start,
+        "sD": ring_c[1].start,
+        "sP": b_start,
+        "sX": x_start,
+        "P1": lambda: gather_b(1),
+        "P2": lambda: gather_b(2),
         "La": lambda: mine_done(3, reduce_a.last()),
-        "Lx": lambda: mine_done(2, reduce_x.last()),
+        "Ly": lambda: mine_done(2, reduce_y.last()),
         "Oa": lambda: other_done(3),
         "Ob": lambda: other_done(2),
     }
     for i in range(1, 5):
         steps[f"A{i}"] = lambda i=i: gather_a(i)
-        steps[f"C{i}"] = lambda i=i: gather_c(i)
+        steps[f"C{i}"] = lambda i=i: ring_c[0].stage(i)
+        steps[f"D{i}"] = lambda i=i: ring_c[1].stage(i)
     for i in range(4):
         steps[f"ab{i}"] = lambda i=i: ab_rows(i)
         steps[f"cb{i}"] = lambda i=i: cb_rows(i)
@@ -463,10 +472,10 @@
         steps[f"bc{i}"] = lambda i=i: b_cols(i)
         steps[f"ns{i}"] = lambda i=i: near_go(i)
     for q in range(2):
-        steps[f"Lb{q}"] = lambda q=q: b_last(q)
+        steps[f"Lx{q}"] = lambda q=q: b_last(q)
         steps[f"Lc{q}"] = lambda q=q: mine_done(q, reduce_c[q].last())
         steps[f"Sc{q}"] = lambda q=q: other_done(q)
-    for name, ring in (("a", reduce_a), ("b0", reduce_b[0]), ("b1", reduce_b[1]), ("c0", reduce_c[0]), ("c1", reduce_c[1]), ("x", reduce_x)):
+    for name, ring in (("a", reduce_a), ("x0", reduce_x[0]), ("x1", reduce_x[1]), ("c0", reduce_c[0]), ("c1", reduce_c[1]), ("y", reduce_y)):
         for way, direction in (("f", ring.far), ("n", -ring.far)):
             for i in range(1, ring.steps(direction) + 1):
                 steps[f"{name}{way}{i}"] = lambda ring=ring, d=direction, i=i: ring.step(d, i)
@@ -501,12 +510,13 @@
     for name in ORDER:
         steps[name]()
 
-    for ring in (ring_a, ring_c, *ring_b, reduce_a, reduce_x, *reduce_c, *reduce_b):
+    for ring in (ring_a, *ring_c, *ring_b, reduce_a, reduce_y, *reduce_c, *reduce_x):
         ring.finish()
-    beside.wait_send()
     for i in range(7):
         pass_over(i, at.c).wait_send()
-        share(i, at.xh).wait_send()
+    for i in range(4):
+        for q in range(2):
+            over_x(i, q).wait_send()
     for i in range(8):
         near(i, 1 - at.c).wait_send()
     for i in range(4):
@@ -543,8 +553,8 @@
             m((2, 2, 7, QUARTER, WIDTH), i16), m((2, 2, 7, 8, 128), f32),
             m((2, 3, QUARTER, WIDTH), i16), m((2, 3, 8, 128), f32),
             m((2, HALF, WIDTH), f32),
-            dma((2, 4)), dma((2, 4)), dma((2, 2, 2)), dma((2, 2, 2)), dma((2, 4)), dma((2, 4)),
-            dma((7,)), dma((7,)), dma((1,)), dma((1,)), dma((7,)), dma((7,)), dma((3,)),
+            dma((2, 4)), dma((2, 4)), dma((2, 2, 2)), dma((2, 2, 2)), dma((2, 2, 4)), dma((2, 2, 4)),
+            dma((7,)), dma((7,)), dma((2, 4)), dma((2, 4)), dma((3,)),
             dma((7, 2)), dma((7, 2)), dma((2, 3, 2)), dma((2, 3, 2)), dma((2, 7, 2)), dma((2, 7, 2)), dma((3, 2)), dma((3, 2)),
             dma((8,)), dma((8,)), dma((12, 2)), dma((12, 2)),
         ],

time: 98.1 us -> 89.6 us (0.913)
  the two profiles are of different devices: /device:TPU:9 before, /device:TPU:1 now
where the time goes in v4:
time: 89.6 us; the launch traced here: 88.9 us
  Pallas kernels  88.3 us (99%)
    pallas_call x1, Pallas kernels, gradients(): pl.pallas_call(kernel, out_shape=(shape((ROWS, WIDTH), i16), shape((ROWS,...  85 us
    pallas_call x1, Pallas kernels, decode(): pl.pallas_call(decode_kernel, out_shape=(out, out, out), in_specs=[vmem]...  3.25 us

profile of v4, /device:TPU:1, one launch (start us, length us, event | category | flops | bytes accessed | tf_op | source)
XLA Modules:
  0.0 88.9 jit_solution(745248737087475688)
XLA Ops:
  0.6 85.0 %shard_map.85 = (s16[192,1024]{1,0:T(8,128)(2,1)}, s16[192,1024]{1,0:T(8,128)(2,1)}, s16[2,192,1024]{2,1,0:T(8,128)(2,1)}, f32[4,8,128]{2,1,0:T(8,128)}, f32[4,8,128]{2,1,0:T(8,128)}, /*index=5*/f32[2,4,8,128]{3,2,1,0:T(8,128)}) custom-call(f32[3]{0:T(128)} %scale.1, f32[3]{0:T(128)} %bias.1, s32[3,12288]{1,0:T(4,128)} %all_ids.1, bf16[192,1024]{1,0:T(8,128)(2,1)} %a_own.1, ...), custom_call_target="tpu_custom_call" | custom-call | tf_op jit(solution)/shard_map/pallas_call | solution.py:537
  85.6 3.3 %shard_map.86 = (f32[192,1024]{1,0:T(8,128)}, f32[192,1024]{1,0:T(8,128)}, f32[192,1024]{1,0:T(8,128)}) custom-call(s16[192,1024]{1,0:T(8,128)(2,1)} %get-tuple-element.9.a, s16[192,1024]{1,0:T(8,128)(2,1)} %get-tuple-element.10.b, s16[2,192,1024]{2,1,0:T(8,128)(2,1)} %get-tuple-element.11.c, f32[4,8,128]{2,1,0:T(8,128)} %get-tuple-element.12.a_unit, ...), custom_call_target="tpu_custom_call" | custom-call | tf_op jit(solution)/shard_map/pallas_call | solution.py:582

commit v5 on v4

--- a/solution.py
+++ b/solution.py
@@ -19,12 +19,12 @@
 OFFSETS = {8: (4, 3, -3, 2, -2, 1, -1, 0), 4: (2, 1, -1, 0)}
 
 ORDER = (
-    "sC", "sP", "sX", "sA", "sD", "P1", "D1", "C1", "P2", "A1", "C2", "A2", "ab2", "D2", "cb3", "A3",
-    "C3", "ab3", "cb2", "ab1", "D3", "A4", "cb1", "C4", "ab0", "ca1", "D4", "cb0", "ca0", "c1f1", "bc1",
-    "bc0", "x0f1", "c0f1", "c0n1", "bc2", "x0n1", "ca2", "c1f2", "ca3", "ac0", "c1n1", "x1f1", "ns0",
-    "c0f2", "af1", "x0f2", "c1f3", "c0n2", "ac1", "c1n2", "ac2", "an1", "ns1", "c1f4", "af2", "Lx0",
-    "yf1", "x1n1", "ns2", "c0f3", "x1f2", "c1n3", "an2", "af3", "c0n3", "c0f4", "yf2", "Lx1", "Lc1",
-    "an3", "yn1", "af4", "Lc0", "Ly", "Sc1", "La", "Sc0", "Ob", "Oa",
+    "sC", "sP", "sX", "sA", "sD", "ids", "P1", "D1", "C1", "P2", "A1", "C2", "A2", "ab2", "D2", "ab3",
+    "cb3", "A3", "C3", "cb2", "D3", "cb1", "ab1", "A4", "C4", "ab0", "ca1", "D4", "cb0", "ca0", "c1f1",
+    "c0n1", "bc0", "bc1", "c0f1", "x0f1", "x1f1", "bc2", "c1n1", "ca2", "c1f2", "ca3", "c0n2", "x1n1",
+    "ac0", "ns0", "x0n1", "c0f2", "af1", "ac2", "c1f3", "x1f2", "x0f2", "an1", "c1n2", "ac1", "ns1",
+    "c0f3", "af2", "c1n3", "ns2", "c1f4", "Lx0", "yf1", "Lx1", "yn1", "c0f4", "c0n3", "Lc1", "an2",
+    "af3", "yf2", "Lc0", "af4", "an3", "Ly", "La", "Sc1", "Sc0", "Ob", "Oa",
 )
 
 
@@ -192,13 +192,12 @@
                 self.parcel(direction, step).sent()
 
 
-def greet(at, meanwhile):
+def greet(at):
     barrier = pltpu.get_barrier_semaphore()
     others = [at.column(-1), at.column(1), at.diagonal(-1), at.diagonal(1), at.row(-1), at.row(1)]
     others += [at.line(-1), at.line(1), at.other_core(), at.twin(), at.twin(True)]
     for device in others:
         pl.semaphore_signal(barrier, inc=1, device_id=device, device_id_type=MESH)
-    meanwhile()
     pl.semaphore_wait(barrier, len(others))
 
 
@@ -223,7 +222,7 @@
 
 
 def kernel(
-    scale, bias, all_ids, a_own, b_own, c_own, a_out, b_out, c_out, a_unit, b_unit, c_unit, ids, ids_t,
+    scale, bias, ids_in, a_own, b_own, c_own, a_out, b_out, c_out, a_unit, b_unit, c_unit, all_ids, ids, ids_t,
     a, b, c, ga, gb, gc, coef_ab, coef_ca, coef_cb,
     a_near, a_box, a_box_scale, b_box, b_box_scale, c_box, c_box_scale, y_box, y_box_scale, sums,
     ga_send, ga_recv, gb_send, gb_recv, gc_send, gc_recv, gt_send, gt_recv, gx_send, gx_recv, own_sem,
@@ -488,6 +487,7 @@
         return [at.column(o)[0] for o in OFFSETS[8]], k
 
     def lay_out_ids():
+        ids_copy.wait()
         ids[...] = jnp.zeros_like(ids)
         lane = lax.broadcasted_iota(jnp.int32, (3, 256), 1)
         row = lax.broadcasted_iota(jnp.int32, (3, 256), 0)
@@ -504,9 +504,12 @@
                 ids[place] = jnp.where(here, moved, ids[place])
         ids_t[...] = jnp.transpose(ids[:, 0:BLOCK])
 
+    ids_copy = pltpu.make_async_copy(ids_in, all_ids, own_sem.at[3])
+    steps["ids"] = lay_out_ids
+    ids_copy.start()
     for copy in own:
         copy.start()
-    greet(at, lay_out_ids)
+    greet(at)
     for name in ORDER:
         steps[name]()
 
@@ -540,10 +543,10 @@
             shape((ROWS, WIDTH), i16), shape((ROWS, WIDTH), i16), shape((2, ROWS, WIDTH), i16),
             shape((4, 8, 128), f32), shape((4, 8, 128), f32), shape((2, 4, 8, 128), f32),
         ),
-        in_specs=[smem, smem, vmem] + [hbm] * 3,
+        in_specs=[smem, smem] + [hbm] * 4,
         out_specs=(vmem,) * 6,
         scratch_shapes=[
-            m((8, 896), jnp.int32), m((BLOCK, 8), jnp.int32),
+            m((3, TOKENS), jnp.int32), m((8, 896), jnp.int32), m((BLOCK, 8), jnp.int32),
             m((BLOCK, WIDTH), bf16), m((BLOCK, WIDTH), bf16), m((BLOCK, WIDTH), bf16),
             m((BLOCK, WIDTH), f32), m((BLOCK, WIDTH), f32), m((BLOCK, WIDTH), f32),
             m((BLOCK, BLOCK), bf16), m((BLOCK, BLOCK), bf16), m((BLOCK, BLOCK), bf16),
@@ -554,7 +557,7 @@
             m((2, 3, QUARTER, WIDTH), i16), m((2, 3, 8, 128), f32),
             m((2, HALF, WIDTH), f32),
             dma((2, 4)), dma((2, 4)), dma((2, 2, 2)), dma((2, 2, 2)), dma((2, 2, 4)), dma((2, 2, 4)),
-            dma((7,)), dma((7,)), dma((2, 4)), dma((2, 4)), dma((3,)),
+            dma((7,)), dma((7,)), dma((2, 4)), dma((2, 4)), dma((4,)),
             dma((7, 2)), dma((7, 2)), dma((2, 3, 2)), dma((2, 3, 2)), dma((2, 7, 2)), dma((2, 7, 2)), dma((3, 2)), dma((3, 2)),
             dma((8,)), dma((8,)), dma((12, 2)), dma((12, 2)),
         ],
@@ -565,25 +568,56 @@
     return decode(a, b, c, a_unit, b_unit, c_unit)
 
 
-def decode_kernel(a, b, c, a_unit, b_unit, c_unit, a_out, b_out, c_out):
-    def value(code, unit):
-        return code.astype(jnp.int32).astype(jnp.float32) * unit[0:1, 0:1]
-
-    for i in range(4):
-        rows = pl.ds(i * QUARTER, QUARTER)
-        a_out[rows, :] = value(a[rows, :], a_unit[i])
-        b_out[rows, :] = value(b[rows, :], b_unit[i])
-        c_out[rows, :] = value(c[0, rows, :], c_unit[0, i]) + value(c[1, rows, :], c_unit[1, i])
+def decode_kernel(
+    a, b, c, a_unit, b_unit, c_unit, a_out, b_out, c_out, codes, units, values, sems
+):
+    jobs = ((a, a_unit, 0), (b, b_unit, 1), (c.at[0], c_unit.at[0], 2), (c.at[1], c_unit.at[1], 3))
+    reads = [
+        (
+            pltpu.make_async_copy(code, codes.at[i], sems.at[0, i]),
+            pltpu.make_async_copy(unit, units.at[i], sems.at[1, i]),
+        )
+        for code, unit, i in jobs
+    ]
+    for pair in reads:
+        for copy in pair:
+            copy.start()
+
+    def value(i, j):
+        code = codes[i, j * QUARTER : (j + 1) * QUARTER, :]
+        return code.astype(jnp.int32).astype(jnp.float32) * units[i, j, 0:1, 0:1]
+
+    writes = []
+    for n, (terms, out) in enumerate((((0,), a_out), ((1,), b_out), ((2, 3), c_out))):
+        for i in terms:
+            for copy in reads[i]:
+                copy.wait()
+        for j in range(4):
+            total = value(terms[0], j)
+            if len(terms) == 2:
+                total = total + value(terms[1], j)
+            values[n, j * QUARTER : (j + 1) * QUARTER, :] = total
+        writes.append(pltpu.make_async_copy(values.at[n], out, sems.at[2, n]))
+        writes[-1].start()
+    for copy in writes:
+        copy.wait()
 
 
 def decode(a, b, c, a_unit, b_unit, c_unit):
-    vmem = pl.BlockSpec(memory_space=pltpu.VMEM)
+    hbm = pl.BlockSpec(memory_space=pl.ANY)
     out = jax.ShapeDtypeStruct((ROWS, WIDTH), jnp.float32)
     return pl.pallas_call(
         decode_kernel,
         out_shape=(out, out, out),
-        in_specs=[vmem] * 6,
-        out_specs=(vmem, vmem, vmem),
+        in_specs=[hbm] * 6,
+        out_specs=(hbm, hbm, hbm),
+        scratch_shapes=[
+            pltpu.VMEM((4, ROWS, WIDTH), jnp.int16),
+            pltpu.VMEM((4, 4, 8, 128), jnp.float32),
+            pltpu.VMEM((3, ROWS, WIDTH), jnp.float32),
+            pltpu.SemaphoreType.DMA((3, 4)),
+        ],
+        compiler_params=pltpu.CompilerParams(vmem_limit_bytes=56 << 20),
     )(a, b, c, a_unit, b_unit, c_unit)
 
 

time: 89.6 us -> 88.3 us (0.985)
  Pallas kernels: 88.3 us -> 87.3 us
where the time goes in v5:
time: 88.3 us; the launch traced here: 88.1 us
  Pallas kernels  87.3 us (99%)
    pallas_call x1, Pallas kernels, gradients(): pl.pallas_call(kernel, out_shape=(shape((ROWS, WIDTH), i16), shape((ROWS,...  84.6 us
    pallas_call x1, Pallas kernels, decode(): pl.pallas_call(decode_kernel, out_shape=(out, out, out), in_specs=[hbm] *...  2.67 us

profile of v5, /device:TPU:1, one launch (start us, length us, event | category | flops | bytes accessed | tf_op | source)
XLA Modules:
  0.0 88.1 jit_solution(8998063361000071002)
XLA Ops:
  0.6 84.6 %shard_map.85 = (s16[192,1024]{1,0:T(8,128)(2,1)}, s16[192,1024]{1,0:T(8,128)(2,1)}, s16[2,192,1024]{2,1,0:T(8,128)(2,1)}, f32[4,8,128]{2,1,0:T(8,128)}, f32[4,8,128]{2,1,0:T(8,128)}, /*index=5*/f32[2,4,8,128]{3,2,1,0:T(8,128)}) custom-call(f32[3]{0:T(128)} %scale.1, f32[3]{0:T(128)} %bias.1, s32[3,12288]{1,0:T(4,128)} %ids_in.1, bf16[192,1024]{1,0:T(8,128)(2,1)} %a_own.1, ...), custom_call_target="tpu_custom_call" | custom-call | tf_op jit(solution)/shard_map/pallas_call | solution.py:540
  85.3 2.7 %shard_map.86 = (f32[192,1024]{1,0:T(8,128)}, f32[192,1024]{1,0:T(8,128)}, f32[192,1024]{1,0:T(8,128)}) custom-call(s16[192,1024]{1,0:T(8,128)(2,1)} %get-tuple-element.9.a, s16[192,1024]{1,0:T(8,128)(2,1)} %get-tuple-element.10.b, s16[2,192,1024]{2,1,0:T(8,128)(2,1)} %get-tuple-element.11.c, f32[4,8,128]{2,1,0:T(8,128)} %get-tuple-element.12.a_unit, ...), custom_call_target="tpu_custom_call" | custom-call | tf_op jit(solution)/shard_map/pallas_call | solution.py:609

commit v6 on v5

--- a/solution.py
+++ b/solution.py
@@ -124,21 +124,19 @@
         self.data = remote(out, into, send.at[0], recv.at[0], device)
         self.scale = remote(out_scale, into_scale, send.at[1], recv.at[1], device)
 
-    def pack(self, value):
+    def go(self):
+        self.scale.start()
+        self.data.start()
+
+    def start(self, value):
         top = jnp.max(jnp.abs(value), axis=0, keepdims=True)
         top = jnp.maximum(jnp.max(top, axis=1, keepdims=True), 1e-30)
+        self.out_scale[...] = jnp.broadcast_to(top * (1 / 32767.0), (8, 128))
+        self.scale.start()
         self.out[...] = (
             jnp.round(value * (32767.0 / top)).astype(jnp.int32).astype(jnp.int16)
         )
-        self.out_scale[...] = jnp.broadcast_to(top * (1 / 32767.0), (8, 128))
-
-    def go(self):
         self.data.start()
-        self.scale.start()
-
-    def start(self, value):
-        self.pack(value)
-        self.go()
 
     def arrive(self):
         self.data.wait_recv()

time: 88.3 us -> 88.3 us (level)
  no operation moved by 1% of the time
where the time goes in v6:
time: 88.3 us; the launch traced here: 88.2 us
  Pallas kernels  87.4 us (99%)
    pallas_call x1, Pallas kernels, gradients(): pl.pallas_call(kernel, out_shape=(shape((ROWS, WIDTH), i16), shape((ROWS,...  84.7 us
    pallas_call x1, Pallas kernels, decode(): pl.pallas_call(decode_kernel, out_shape=(out, out, out), in_specs=[hbm] *...  2.67 us

profile of v6, /device:TPU:1, one launch (start us, length us, event | category | flops | bytes accessed | tf_op | source)
XLA Modules:
  0.0 88.2 jit_solution(3867481846269462459)
XLA Ops:
  0.6 84.7 %shard_map.85 = (s16[192,1024]{1,0:T(8,128)(2,1)}, s16[192,1024]{1,0:T(8,128)(2,1)}, s16[2,192,1024]{2,1,0:T(8,128)(2,1)}, f32[4,8,128]{2,1,0:T(8,128)}, f32[4,8,128]{2,1,0:T(8,128)}, /*index=5*/f32[2,4,8,128]{3,2,1,0:T(8,128)}) custom-call(f32[3]{0:T(128)} %scale.1, f32[3]{0:T(128)} %bias.1, s32[3,12288]{1,0:T(4,128)} %ids_in.1, bf16[192,1024]{1,0:T(8,128)(2,1)} %a_own.1, ...), custom_call_target="tpu_custom_call" | custom-call | tf_op jit(solution)/shard_map/pallas_call | solution.py:538
  85.3 2.7 %shard_map.86 = (f32[192,1024]{1,0:T(8,128)}, f32[192,1024]{1,0:T(8,128)}, f32[192,1024]{1,0:T(8,128)}) custom-call(s16[192,1024]{1,0:T(8,128)(2,1)} %get-tuple-element.9.a, s16[192,1024]{1,0:T(8,128)(2,1)} %get-tuple-element.10.b, s16[2,192,1024]{2,1,0:T(8,128)(2,1)} %get-tuple-element.11.c, f32[4,8,128]{2,1,0:T(8,128)} %get-tuple-element.12.a_unit, ...), custom_call_target="tpu_custom_call" | custom-call | tf_op jit(solution)/shard_map/pallas_call | solution.py:607
